TPU v7x, 512 devices: a whole 4x4x16 slice. The times are simulated.
512 devices in a mesh: row: 32 (over z, y_lo), col: 16 (over y_hi, x, core).
Axes of the slice: x: 4, y: 4 (y_hi: 2, y_lo: 2; y = y_hi * 2 + y_lo), z: 16, core: 2. Of those that a mesh axis runs over, the one named last changes fastest.
Arguments:
- slab_t: bfloat16 [2, 1024, 98304], P(None, 'col', 'row'), may hold values from -6 to 6
- target_t: bfloat16 [2, 1024, 98304], P(None, 'col', 'row'), may hold values from -6 to 6
- factor_h: bfloat16 [2, 1024, 1024], P(None, 'row', 'col'), may hold values from -0.1875 to 0.1875
Outputs:
- gram_residual: float32 [1024, 2, 1024], P('row', None, 'col')
- polar_residual: float32 [2, 1024, 98304], P(None, 'col', 'row')
All inputs are finite; a program needn't handle non-finite values.
Results may differ from a plain program's by a relative error of at most 0.0003.
Values may be sent and summed in bfloat16 or wider, within the bound.
No kernel may reach another device: no remote copies, remote signals or barrier semaphores. Data moves between devices by JAX's collectives and lax.ppermute only.
A program may use at most 64 MiB of HBM per device.

v0:
```python
import math

import jax
import jax.numpy as jnp
from jax import lax
from jax.sharding import PartitionSpec as P


def shards(slab_t, target_t, factor_h):
    hcols = lax.all_gather(factor_h, "row", axis=1, tiled=True)
    slabs, width_loc, nb_loc = slab_t.shape
    width_all = hcols.shape[1]
    col_index = lax.axis_index("col")
    piece = lax.all_gather(slab_t, "col", axis=1, tiled=True)
    partial_f = jnp.einsum("skj,skn->sjn", hcols, piece, preferred_element_type=jnp.float32)
    block = jnp.einsum("sbn,san->bsa", piece, slab_t, preferred_element_type=jnp.float32)
    partial_f, terms = (partial_f, block)
    nrows_row = lax.axis_size("row")
    local_rows = width_all // nrows_row
    summed = lax.psum_scatter(terms, "row", scatter_dimension=0, tiled=True)
    order_n = nb_loc * nrows_row
    b_index = lax.axis_index("row") * local_rows + jnp.arange(local_rows, dtype=jnp.int32)
    a_index = col_index * width_loc + jnp.arange(width_loc, dtype=jnp.int32)
    identity = (b_index[:, None, None] == a_index[None, None, :]).astype(jnp.float32)
    gram = (summed - order_n * identity) * (1.0 / math.sqrt(order_n))
    polar = target_t.astype(jnp.float32) - partial_f
    return (gram, polar)


def solution(mesh):
    return jax.shard_map(
        shards,
        mesh=mesh,
        in_specs=(P(None, "col", "row"), P(None, "col", "row"), P(None, "row", "col")),
        out_specs=(P("row", None, "col"), P(None, "col", "row")),
        check_vma=False,
    )
```

profile of v0, /device:TPU:6, one launch (start us, length us, event | category | flops | bytes accessed | tf_op | source)
XLA Modules:
  0.0 406.4 jit_solution(10443460925206244931)
XLA Ops:
  7.2 0.0 copy-start
  7.2 0.0 all-gather.2.cloned.1.call-start
  7.2 0.7 all-gather.2.cloned.1.call-update
  7.9 0.0 all-reduce.3.cloned.1.call-start
  8.0 1.3 dynamic-slice
  9.9 73.0 %all_gather.7 = bf16[2,1024,64]{2,1,0:T(8,128)(2,1)S(1)} all-gather(bf16[2,32,64]{2,1,0:T(8,128)(2,1)} %param.5), channel_id=1, replica_groups=mesh['row'=32,'col'=16] {'row'}, dimensions={1}, use_global_device_ids=true | all-gather | bytes 270336 | tf_op jit(solution)/shard_map/all_gather | solution.py:10
  82.9 0.1 compare_select_fusion
  83.0 39.7 %all-gather.2.cloned.1.call-done = bf16[2,1024,3072]{2,1,0:T(8,128)(2,1)} async-done(((bf16[2,64,3072]{2,1,0:T(8,128)(2,1)}), bf16[2,1024,3072]{2,1,0:T(8,128)(2,1)}) %all-gather.2.cloned.1.call-update) | async-done | bytes 12582928 | tf_op jit(solution)/shard_map/all_gather | solution.py:14
  122.6 8.8 %convolution_bitcast_fusion = f32[1024,2,64]{0,2,1:T(8,128)S(1)} fusion(bf16[2,64,3072]{2,1,0:T(8,128)(2,1)} %param.3, bf16[2,1024,3072]{2,1,0:T(8,128)(2,1)} %all-gather.2.cloned.1.call-done), kind=kOutput, calls=%fused_computation.1 | convolution fusion | flops 805306368 | bytes 13893632 | tf_op jit(solution)/shard_map/sbn,san->bsa/dot_general | solution.py:16
  131.4 1.3 copy.6
  132.7 0.0 all-reduce.3.cloned.1.call-update
  132.7 0.0 copy-done
  132.7 8.1 %convolution_subtract_fusion = f32[2,64,3072]{2,1,0:T(8,128)} fusion(bf16[2,1024,64]{2,1,0:T(8,128)(2,1)S(1)} %all_gather.7, bf16[2,1024,3072]{2,1,0:T(8,128)(2,1)} %all-gather.2.cloned.1.call-done, bf16[2,64,3072]{2,1,0:T(8,128)(2,1)S(1)} %copy-done), kind=kOutput, calls=%fused_computation | convolution fusion | flops 806092800 | bytes 15204352 | tf_op jit(solution)/shard_map/skj,skn->sjn/dot_general | solution.py:15
  140.8 257.4 %all-reduce.3.cloned.1.call-done = f32[1024,2,64]{2,1,0:T(2,128)} async-done(((f32[1024,2,64]{2,1,0:T(2,128)}), f32[1024,2,64]{2,1,0:T(2,128)}) %all-reduce.3.cloned.1.call-update) | async-done | bytes 524304
  398.2 1.4 fusion
  (2 shorter events, 0.0 us)
Async XLA Ops:
  7.2 125.5 %copy-start = (bf16[2,64,3072]{2,1,0:T(8,128)(2,1)S(1)}, bf16[2,64,3072]{2,1,0:T(8,128)(2,1)}, u32[]{:S(2)}) copy-start(bf16[2,64,3072]{2,1,0:T(8,128)(2,1)} %param.4) | copy-start | bytes 2359300
  7.2 115.5 %all-gather.2.cloned.1.call-start = ((), (), s32[]{:S(2)}) async-start(), calls=%async_computation | async-start | bytes 13369344 | tf_op jit(solution)/shard_map/all_gather | solution.py:14
  7.9 390.3 %all-reduce.3.cloned.1.call-start = ((), (), s32[]{:S(2)}) async-start(), calls=%async_computation.1 | async-start | bytes 2097152
Sparse Core Ops, SparseCore 0:
  11.4 111.2 all-gather.1
  132.8 265.3 all-reduce.2
where the time goes:
time: 407 us; the launch traced here: 406 us
  waiting for transfers between devices  298 us (73%)
  blocking collectives  73 us (18%)
  matrix products  16.8 us (4%)
  between operations  14.7 us (4%)
    unnamed x3, waiting for transfers between devices  258 us
    all_gather x1, blocking collectives, shards(): hcols = lax.all_gather(factor_h, 'row', axis=1, tiled=True)  73 us
    all_gather x1, waiting for transfers between devices, shards(): piece = lax.all_gather(slab_t, 'col', axis=1, tiled=True)  39.7 us
    dot_general x1, matrix products, shards(): jnp.einsum('sbn,san->bsa', piece, slab_t, preferred_element_type=jnp.floa...  8.75 us
  transfers between devices with their start and end apart: 2, of which 2 were waited for; matrix products, arithmetic and copies ran while one was open for 2% of the time, Pallas kernels for 0%

commit v1 on v0

v1 whole, which is shorter than its diff:
```python
import math

import jax
import jax.numpy as jnp
from jax import lax
from jax.experimental import pallas as pl
from jax.experimental.pallas import tpu as pltpu
from jax.sharding import Mesh, PartitionSpec as P

AXES = ("z", "yl", "yh", "x", "c")
ROW = ("z", "yl")
COL = ("yh", "x", "c")
SWAP = [(0, 1), (1, 0)]


def shift(a, by):
    return lax.ppermute(a, "x", [(i, (i + by) % 4) for i in range(4)])


def products(index, own, a_mine, a_core, b_mine, b_core, h, recon, gram):
    width = 64
    mine = own[...]
    total = None
    for at, rows in enumerate((a_mine, a_core, b_mine, b_core)):
        block = rows[...]
        terms = lax.dot_general(block, mine, (((1,), (1,)), ((), ())), preferred_element_type=jnp.float32)
        picked = []
        for part in range(4):
            place = pl.ds(pl.multiple_of(index[at * 4 + part] * width, width), width)
            gram[place, :] = terms[part * width:(part + 1) * width]
            picked.append(h[place, :])
        factor = jnp.concatenate(picked, axis=0)
        term = lax.dot_general(factor, block, (((0,), (0,)), ((), ())), preferred_element_type=jnp.float32)
        if total is None:
            total = term
        else:
            total = total + term
    recon[...] = total


def shards(slab_t, target_t, factor_h):
    yh, x, c = (lax.axis_index(name) for name in COL)
    width, rows = slab_t.shape[1:]

    def pick(array, at):
        return lax.dynamic_index_in_dim(array, at, 0, keepdims=False)

    own = pick(slab_t, yh)
    other = lax.ppermute(pick(slab_t, 1 - yh), "yh", SWAP)
    h_other = lax.ppermute(pick(factor_h, 1 - yh), "yh", SWAP)
    h_mine = jnp.concatenate([pick(factor_h, yh), h_other], axis=1)

    def over_x(a):
        return jnp.concatenate([a, shift(a, 1), shift(a, -1), shift(a, 2)], axis=0)

    a_mine = over_x(own)
    b_mine = over_x(other)
    nrow = lax.axis_size(ROW)
    h_all = lax.all_to_all(jnp.broadcast_to(h_mine[None], (nrow,) + h_mine.shape), ROW, 0, 0, tiled=True)
    h_all = h_all.reshape(-1, 2 * width)
    a_core = lax.ppermute(a_mine, "c", SWAP)
    b_core = lax.ppermute(b_mine, "c", SWAP)

    at_x = jnp.stack([x, (x + 3) % 4, (x + 1) % 4, (x + 2) % 4])
    at_yc = jnp.stack([yh * 8 + c, yh * 8 + 1 - c, 8 - yh * 8 + c, 9 - yh * 8 - c])
    index = (at_yc[:, None] + 2 * at_x[None, :]).reshape(16).astype(jnp.int32)

    vmem = pl.BlockSpec(memory_space=pltpu.VMEM)
    recon, terms = pl.pallas_call(
        products,
        out_shape=(
            jax.ShapeDtypeStruct((2 * width, rows), jnp.float32),
            jax.ShapeDtypeStruct((16 * width, 2 * width), jnp.float32),
        ),
        in_specs=[pl.BlockSpec(memory_space=pltpu.SMEM)] + [vmem] * 6,
        out_specs=(vmem, vmem),
        compiler_params=pltpu.CompilerParams(vmem_limit_bytes=40 * 2**20),
        cost_estimate=pl.CostEstimate(flops=4 * 16 * 2 * width * width * rows, bytes_accessed=10 * 2**20, transcendentals=0),
    )(index, jnp.concatenate([own, other], axis=0), a_mine, a_core, b_mine, b_core, h_all)

    slab = jnp.arange(2, dtype=jnp.int32)
    recon_other = lax.ppermute(recon[width:], "yh", SWAP)
    is_own = (slab == yh)[:, None, None]
    polar = target_t.astype(jnp.float32) - jnp.where(is_own, recon[None, :width], recon_other[None])

    local = 16 * width // nrow
    summed = lax.all_to_all(terms.reshape(nrow, local, 2 * width), ROW, 0, 0, tiled=True).sum(0)
    gram_other = lax.ppermute(summed[:, width:], "yh", SWAP)
    gram = jnp.where((slab == yh)[None, :, None], summed[:, None, :width], gram_other[:, None])
    order_n = rows * nrow
    b_index = lax.axis_index(ROW) * local + jnp.arange(local, dtype=jnp.int32)
    a_index = lax.axis_index(COL) * width + jnp.arange(width, dtype=jnp.int32)
    identity = (b_index[:, None, None] == a_index[None, None, :]).astype(jnp.float32)
    gram = (gram - order_n * identity) * (1.0 / math.sqrt(order_n))
    return (gram, polar)


def solution(mesh):
    parts = Mesh(mesh.devices.reshape(16, 2, 2, 4, 2), AXES)
    return jax.shard_map(
        shards,
        mesh=parts,
        in_specs=(P(None, COL, ROW), P(None, COL, ROW), P(None, ROW, COL)),
        out_specs=(P(ROW, None, COL), P(None, COL, ROW)),
        check_vma=False,
    )
```

time: 407 us -> 156 us (0.38)
  waiting for transfers between devices: 298 us -> 77.4 us
  blocking collectives: 73 us -> 0 us
  starting transfers between devices: 0.08 us -> 59.3 us
  matrix products: 16.8 us -> 0 us
  between operations: 14.7 us -> 0.94 us
  Pallas kernels: 0 us -> 5.57 us
  local copies, waits for them, and re-layouts: 2.54 us -> 7.87 us
    unnamed x3 -> x0, waiting for transfers between devices: 258 us -> none
    all_gather x1 -> x0, blocking collectives: 73 us -> none  [shards(): hcols = lax.all_gather(factor_h, 'row', axis=1, tiled=True)]
    all_to_all x0 -> x2, waiting for transfers between devices: none -> 47.3 us  [the longest x1 26.2 us: shards(): lax.all_to_all(terms.reshape(nrow, local, 2 * width), ROW, 0, 0, tiled=True)]
    ppermute x0 -> x12, starting transfers between devices: none -> 39.8 us  [the longest x6 20.1 us: shift(): return lax.ppermute(a, 'x', [(i, (i + by) % 4) for i in range(4)])]
    all_gather x1 -> x0, waiting for transfers between devices: 39.7 us -> none  [shards(): piece = lax.all_gather(slab_t, 'col', axis=1, tiled=True)]
    ppermute x0 -> x12, waiting for transfers between devices: none -> 30.1 us  [the longest x6 25.6 us: shift(): return lax.ppermute(a, 'x', [(i, (i + by) % 4) for i in range(4)])]
    all_to_all x0 -> x2, starting transfers between devices: none -> 19.5 us  [the longest x1 15.6 us: shards(): lax.all_to_all(jnp.broadcast_to(h_mine[None], (nrow,) + h_mine.shape), RO...]
    dot_general x2 -> x0, matrix products: 16.8 us -> none  [the longest x1 8.75 us: shards(): jnp.einsum('sbn,san->bsa', piece, slab_t, preferred_element_type=jnp.floa...]
  transfers between devices with their start and end apart: 2 -> 14, of which waited for: 2 -> 7; matrix products, arithmetic and copies ran while one was open for 2% -> 6% of each run, Pallas kernels for 0% -> 0%
where the time goes in v1:
time: 156 us; the launch traced here: 155 us
  waiting for transfers between devices  77.4 us (50%)
  starting transfers between devices  59.3 us (38%)
  local copies, waits for them, and re-layouts  7.87 us (5%)
  Pallas kernels  5.57 us (4%)
  other arithmetic  3.78 us (2%)
    all_to_all x1, waiting for transfers between devices, shards(): lax.all_to_all(terms.reshape(nrow, local, 2 * width), ROW, 0, 0, tiled=True)  26.2 us
    ppermute x6, waiting for transfers between devices, shift(): return lax.ppermute(a, 'x', [(i, (i + by) % 4) for i in range(4)])  25.6 us
    all_to_all x1, waiting for transfers between devices, shards(): lax.all_to_all(jnp.broadcast_to(h_mine[None], (nrow,) + h_mine.shape), RO...  21 us
    ppermute x6, starting transfers between devices, shift(): return lax.ppermute(a, 'x', [(i, (i + by) % 4) for i in range(4)])  20.1 us
    all_to_all x1, starting transfers between devices, shards(): lax.all_to_all(jnp.broadcast_to(h_mine[None], (nrow,) + h_mine.shape), RO...  15.6 us
    pallas_call x1, Pallas kernels, shards(): pl.pallas_call(products, out_shape=(jax.ShapeDtypeStruct((2 * width, rows...  5.57 us
    ppermute x1, starting transfers between devices, shards(): other = lax.ppermute(pick(slab_t, 1 - yh), 'yh', SWAP)  5.1 us
    all_to_all x1, starting transfers between devices, shards(): lax.all_to_all(terms.reshape(nrow, local, 2 * width), ROW, 0, 0, tiled=True)  3.89 us
  transfers between devices with their start and end apart: 14, of which 7 were waited for; matrix products, arithmetic and copies ran while one was open for 6% of the time, Pallas kernels for 0%

profile of v1, /device:TPU:6, one launch (start us, length us, event | category | flops | bytes accessed | tf_op | source)
XLA Modules:
  0.0 154.8 jit_solution(13125330862260058878)
XLA Ops:
  0.6 1.2 dynamic-slice_bitcast_fusion.1
  1.8 5.1 %collective-permute-start = (bf16[64,3072]{1,0:T(8,128)(2,1)S(1)}, bf16[64,3072]{1,0:T(8,128)(2,1)S(1)}, u32[]{:S(2)}, u32[]{:S(2)}) collective-permute-start(bf16[64,3072]{1,0:T(8,128)(2,1)S(1)} %get-tuple-element.9), channel_id=1, source_target_pairs={{0,8},{8,0},{1,9},{9,1},{2,10},{10,2},{3,11},{11,3},{4,12},{12,4},... | collective-permute-start | bytes 1179656 | tf_op jit(solution)/shard_map/ppermute | solution.py:49
  6.9 4.6 %collective-permute-start.1 = (bf16[64,3072]{1,0:T(8,128)(2,1)S(1)}, bf16[64,3072]{1,0:T(8,128)(2,1)S(1)}, u32[]{:S(2)}, u32[]{:S(2)}) collective-permute-start(bf16[64,3072]{1,0:T(8,128)(2,1)S(1)} %get-tuple-element.8), channel_id=1, source_target_pairs={{0,2},{2,4},{4,6},{6,0},{1,3},{3,5},{5,7},{7,1},{8,10},{10,12},{12... | collective-permute-start | bytes 1179656 | tf_op jit(solution)/shard_map/ppermute | solution.py:17
  11.5 1.9 %collective-permute-start.2 = (bf16[64,3072]{1,0:T(8,128)(2,1)S(1)}, bf16[64,3072]{1,0:T(8,128)(2,1)S(1)}, u32[]{:S(2)}, u32[]{:S(2)}) collective-permute-start(bf16[64,3072]{1,0:T(8,128)(2,1)S(1)} %get-tuple-element.8), channel_id=1, source_target_pairs={{0,6},{2,0},{4,2},{6,4},{1,7},{3,1},{5,3},{7,5},{8,14},{10,8},{12,... | collective-permute-start | bytes 1179656 | tf_op jit(solution)/shard_map/ppermute | solution.py:17
  13.4 3.4 %collective-permute-start.3 = (bf16[64,3072]{1,0:T(8,128)(2,1)S(1)}, bf16[64,3072]{1,0:T(8,128)(2,1)S(1)}, u32[]{:S(2)}, u32[]{:S(2)}) collective-permute-start(bf16[64,3072]{1,0:T(8,128)(2,1)S(1)} %get-tuple-element.8), channel_id=1, source_target_pairs={{0,4},{2,6},{4,0},{6,2},{1,5},{3,7},{5,1},{7,3},{8,12},{10,14},{12... | collective-permute-start | bytes 1179656 | tf_op jit(solution)/shard_map/ppermute | solution.py:17
  16.8 0.0 collective-permute-done
  16.8 3.9 %collective-permute-start.5 = (bf16[64,3072]{1,0:T(8,128)(2,1)S(1)}, bf16[64,3072]{1,0:T(8,128)(2,1)S(1)}, u32[]{:S(2)}, u32[]{:S(2)}) collective-permute-start(bf16[64,3072]{1,0:T(8,128)(2,1)S(1)} %collective-permute-done), channel_id=1, source_target_pairs={{0,2},{2,4},{4,6},{6,0},{1,3},{3,5},{5,7},{7,1},{8,10},{10,12},{12... | collective-permute-start | bytes 1179656 | tf_op jit(solution)/shard_map/ppermute | solution.py:17
  20.7 0.1 collective-permute-done.1
  20.9 10.3 %collective-permute-done.2 = bf16[64,3072]{1,0:T(8,128)(2,1)S(1)} collective-permute-done((bf16[64,3072]{1,0:T(8,128)(2,1)S(1)}, bf16[64,3072]{1,0:T(8,128)(2,1)S(1)}, u32[]{:S(2)}, u32[]{:S(2)}) %collective-permute-start.2) | collective-permute-done | bytes 393248 | tf_op jit(solution)/shard_map/ppermute | solution.py:17
  31.1 0.0 collective-permute-done.3
  31.1 0.1 pad_maximum_fusion.a_mine
  31.2 0.0 copy-start.2
  31.3 1.9 %collective-permute-start.4 = (bf16[256,3072]{1,0:T(8,128)(2,1)S(1)}, bf16[256,3072]{1,0:T(8,128)(2,1)}, u32[]{:S(2)}, u32[]{:S(2)}) collective-permute-start(bf16[256,3072]{1,0:T(8,128)(2,1)S(1)} %pad_maximum_fusion.a_mine), channel_id=1, source_target_pairs={{0,1},{1,0},{2,3},{3,2},{4,5},{5,4},{6,7},{7,6},{8,9},{9,8},{10,11... | collective-permute-start | bytes 4718600 | tf_op jit(solution)/shard_map/ppermute | solution.py:61
  33.2 1.9 %collective-permute-start.6 = (bf16[64,3072]{1,0:T(8,128)(2,1)S(1)}, bf16[64,3072]{1,0:T(8,128)(2,1)S(1)}, u32[]{:S(2)}, u32[]{:S(2)}) collective-permute-start(bf16[64,3072]{1,0:T(8,128)(2,1)S(1)} %collective-permute-done), channel_id=1, source_target_pairs={{0,6},{2,0},{4,2},{6,4},{1,7},{3,1},{5,3},{7,5},{8,14},{10,8},{12,... | collective-permute-start | bytes 1179656 | tf_op jit(solution)/shard_map/ppermute | solution.py:17
  35.1 0.8 constant_dynamic-update-slice_fusion.3
  35.9 4.4 %collective-permute-start.7 = (bf16[64,3072]{1,0:T(8,128)(2,1)S(1)}, bf16[64,3072]{1,0:T(8,128)(2,1)S(1)}, u32[]{:S(2)}, u32[]{:S(2)}) collective-permute-start(bf16[64,3072]{1,0:T(8,128)(2,1)S(1)} %collective-permute-done), channel_id=1, source_target_pairs={{0,4},{2,6},{4,0},{6,2},{1,5},{3,7},{5,1},{7,3},{8,12},{10,14},{12... | collective-permute-start | bytes 1179656 | tf_op jit(solution)/shard_map/ppermute | solution.py:17
  40.3 0.8 constant_dynamic-update-slice_fusion.2
  41.0 15.2 %collective-permute-done.6 = bf16[64,3072]{1,0:T(8,128)(2,1)S(1)} collective-permute-done((bf16[64,3072]{1,0:T(8,128)(2,1)S(1)}, bf16[64,3072]{1,0:T(8,128)(2,1)S(1)}, u32[]{:S(2)}, u32[]{:S(2)}) %collective-permute-start.6) | collective-permute-done | bytes 393248 | tf_op jit(solution)/shard_map/ppermute | solution.py:17
  56.2 0.8 constant_dynamic-update-slice_fusion.1
  57.0 0.0 collective-permute-done.7
  57.0 0.8 constant_dynamic-update-slice_fusion.b_mine
  57.8 1.9 %collective-permute-start.8 = (bf16[256,3072]{1,0:T(8,128)(2,1)}, bf16[256,3072]{1,0:T(8,128)(2,1)}, u32[]{:S(2)}, u32[]{:S(2)}) collective-permute-start(bf16[256,3072]{1,0:T(8,128)(2,1)} %constant_dynamic-update-slice_fusion.b_mine), channel_id=1, source_target_pairs={{0,1},{1,0},{2,3},{3,2},{4,5},{5,4},{6,7},{7,6},{8,9},{9,8},{10,11... | collective-permute-start | bytes 4718600 | tf_op jit(solution)/shard_map/ppermute | solution.py:62
  59.7 3.4 %collective-permute-start.9 = (bf16[32,64]{1,0:T(8,128)(2,1)S(1)}, bf16[32,64]{1,0:T(8,128)(2,1)S(1)}, u32[]{:S(2)}, u32[]{:S(2)}) collective-permute-start(bf16[32,64]{1,0:T(8,128)(2,1)S(1)} %get-tuple-element.13), channel_id=1, source_target_pairs={{0,8},{8,0},{1,9},{9,1},{2,10},{10,2},{3,11},{11,3},{4,12},{12,4},... | collective-permute-start | bytes 12296 | tf_op jit(solution)/shard_map/ppermute | solution.py:50
  63.1 3.7 %collective-permute-done.9 = bf16[32,64]{1,0:T(8,128)(2,1)S(1)} collective-permute-done((bf16[32,64]{1,0:T(8,128)(2,1)S(1)}, bf16[32,64]{1,0:T(8,128)(2,1)S(1)}, u32[]{:S(2)}, u32[]{:S(2)}) %collective-permute-start.9) | collective-permute-done | bytes 4128 | tf_op jit(solution)/shard_map/ppermute | solution.py:50
  66.8 0.1 pad_maximum_fusion.2
  66.9 0.7 broadcast_in_dim.65
  67.6 15.6 %all-to-all-start = ((bf16[32,32,128]{2,1,0:T(8,128)(2,1)}), bf16[32,32,128]{2,1,0:T(8,128)(2,1)S(1)}, u32[]{:S(2)}, u32[]{:S(2)}) async-start(bf16[32,32,128]{2,1,0:T(8,128)(2,1)} %broadcast_in_dim.65), calls=%async_computation | async-start | bytes 524288 | tf_op jit(solution)/shard_map/all_to_all | solution.py:59
  83.2 0.1 pad_add_fusion
  83.3 0.1 broadcast_add_fusion
  83.4 0.1 add.97.index
  83.5 0.1 pad_maximum_fusion.1.own
  83.5 21.0 %all-to-all-done = bf16[32,32,128]{2,1,0:T(8,128)(2,1)S(1)} async-done(((bf16[32,32,128]{2,1,0:T(8,128)(2,1)}), bf16[32,32,128]{2,1,0:T(8,128)(2,1)S(1)}, u32[]{:S(2)}, u32[]{:S(2)}) %all-to-all-start) | async-done | bytes 262176 | tf_op jit(solution)/shard_map/all_to_all | solution.py:59
  104.6 0.0 collective-permute-done.4.a_core
  104.6 0.0 collective-permute-done.8.b_core
  104.6 5.6 %shard_map.50 = (f32[128,3072]{1,0:T(8,128)S(1)}, f32[1024,128]{1,0:T(8,128)}) custom-call(s32[16]{0:T(128)S(1)} %add.97.index, bf16[128,3072]{1,0:T(8,128)(2,1)S(1)} %pad_maximum_fusion.1.own, bf16[256,3072]{1,0:T(8,128)(2,1)S(1)} %pad_maximum_fusion.a_mine, bf16[256,3072]{1,0:T(8,128)(2,1)} %collective-permute-done.4.a_core, ...), custom_call_target="tpu_custom_call" | custom-call | flops 1610612736 | bytes 10485760 | tf_op jit(solution)/shard_map/pallas_call | solution.py:69
  110.2 1.1 copy-done
  111.3 3.9 %all-to-all-start.1 = ((f32[32,32,128]{2,1,0:T(8,128)}), f32[32,32,128]{2,1,0:T(8,128)S(1)}, u32[]{:S(2)}, u32[]{:S(2)}) async-start(f32[32,32,128]{2,1,0:T(8,128)} %bitcast.13), calls=%async_computation.1 | async-start | bytes 1048576 | tf_op jit(solution)/shard_map/all_to_all | solution.py:87
  115.2 0.0 copy-start.1
  115.2 1.6 %fusion = (f32[64,3072]{1,0:T(8,128)S(1)}, f32[64,3072]{1,0:T(8,128)S(1)}) fusion(f32[128,3072]{1,0:T(8,128)} %copy-done), kind=kLoop, calls=%fused_computation.20 | loop fusion | bytes 3145728 | tf_op jit(solution)/shard_map/slice | solution.py:84
  116.8 3.7 %collective-permute-start.11 = (f32[64,3072]{1,0:T(8,128)S(1)}, f32[64,3072]{1,0:T(8,128)}, u32[]{:S(2)}, u32[]{:S(2)}) collective-permute-start(f32[64,3072]{1,0:T(8,128)S(1)} %get-tuple-element.7), channel_id=1, source_target_pairs={{0,8},{8,0},{1,9},{9,1},{2,10},{10,2},{3,11},{11,3},{4,12},{12,4},... | collective-permute-start | bytes 2359304 | tf_op jit(solution)/shard_map/ppermute | solution.py:82
  120.6 0.1 compare_select_fusion
  120.7 26.2 %all-to-all-done.1 = f32[32,32,128]{2,1,0:T(8,128)S(1)} async-done(((f32[32,32,128]{2,1,0:T(8,128)}), f32[32,32,128]{2,1,0:T(8,128)S(1)}, u32[]{:S(2)}, u32[]{:S(2)}) %all-to-all-start.1) | async-done | bytes 524320 | tf_op jit(solution)/shard_map/all_to_all | solution.py:87
  146.9 0.1 fusion.1
  147.0 3.7 %collective-permute-start.10 = (f32[32,64]{1,0:T(8,128)S(1)}, f32[32,64]{1,0:T(8,128)S(1)}, u32[]{:S(2)}, u32[]{:S(2)}) collective-permute-start(f32[32,64]{1,0:T(8,128)S(1)} %get-tuple-element.11), channel_id=1, source_target_pairs={{0,8},{8,0},{1,9},{9,1},{2,10},{10,2},{3,11},{11,3},{4,12},{12,4},... | collective-permute-start | bytes 24584 | tf_op jit(solution)/shard_map/ppermute | solution.py:88
  150.8 0.0 collective-permute-done.11
  150.8 2.6 %select_subtract_fusion = f32[2,64,3072]{2,1,0:T(8,128)} fusion(bf16[2,64,3072]{2,1,0:T(8,128)(2,1)S(1)} %copy-done.1, f32[64,3072]{1,0:T(8,128)} %collective-permute-done.11, f32[64,3072]{1,0:T(8,128)S(1)} %get-tuple-element.6, pred[2]{0:T(512)(128)(4,1)S(1)} %iota_compare_fusion), kind=kLoop, calls=%fused_computation.1 | loop fusion | flops 1179648 | bytes 3932162 | tf_op jit(solution)/shard_map/sub | solution.py:84
  153.3 0.8 collective-permute-done.10
  154.1 0.7 subtract_multiply_fusion
  (9 shorter events, 0.1 us)
Async XLA Ops:
  1.8 15.0 %collective-permute-start = (bf16[64,3072]{1,0:T(8,128)(2,1)S(1)}, bf16[64,3072]{1,0:T(8,128)(2,1)S(1)}, u32[]{:S(2)}, u32[]{:S(2)}) collective-permute-start(bf16[64,3072]{1,0:T(8,128)(2,1)S(1)} %get-tuple-element.9), channel_id=1, source_target_pairs={{0,8},{8,0},{1,9},{9,1},{2,10},{10,2},{3,11},{11,3},{4,12},{12,4},... | collective-permute-start | bytes 1179656 | tf_op jit(solution)/shard_map/ppermute | solution.py:49
  6.9 13.9 %collective-permute-start.1 = (bf16[64,3072]{1,0:T(8,128)(2,1)S(1)}, bf16[64,3072]{1,0:T(8,128)(2,1)S(1)}, u32[]{:S(2)}, u32[]{:S(2)}) collective-permute-start(bf16[64,3072]{1,0:T(8,128)(2,1)S(1)} %get-tuple-element.8), channel_id=1, source_target_pairs={{0,2},{2,4},{4,6},{6,0},{1,3},{3,5},{5,7},{7,1},{8,10},{10,12},{12... | collective-permute-start | bytes 1179656 | tf_op jit(solution)/shard_map/ppermute | solution.py:17
  11.5 19.6 %collective-permute-start.2 = (bf16[64,3072]{1,0:T(8,128)(2,1)S(1)}, bf16[64,3072]{1,0:T(8,128)(2,1)S(1)}, u32[]{:S(2)}, u32[]{:S(2)}) collective-permute-start(bf16[64,3072]{1,0:T(8,128)(2,1)S(1)} %get-tuple-element.8), channel_id=1, source_target_pairs={{0,6},{2,0},{4,2},{6,4},{1,7},{3,1},{5,3},{7,5},{8,14},{10,8},{12,... | collective-permute-start | bytes 1179656 | tf_op jit(solution)/shard_map/ppermute | solution.py:17
  13.4 17.7 %collective-permute-start.3 = (bf16[64,3072]{1,0:T(8,128)(2,1)S(1)}, bf16[64,3072]{1,0:T(8,128)(2,1)S(1)}, u32[]{:S(2)}, u32[]{:S(2)}) collective-permute-start(bf16[64,3072]{1,0:T(8,128)(2,1)S(1)} %get-tuple-element.8), channel_id=1, source_target_pairs={{0,4},{2,6},{4,0},{6,2},{1,5},{3,7},{5,1},{7,3},{8,12},{10,14},{12... | collective-permute-start | bytes 1179656 | tf_op jit(solution)/shard_map/ppermute | solution.py:17
  16.8 23.4 %collective-permute-start.5 = (bf16[64,3072]{1,0:T(8,128)(2,1)S(1)}, bf16[64,3072]{1,0:T(8,128)(2,1)S(1)}, u32[]{:S(2)}, u32[]{:S(2)}) collective-permute-start(bf16[64,3072]{1,0:T(8,128)(2,1)S(1)} %collective-permute-done), channel_id=1, source_target_pairs={{0,2},{2,4},{4,6},{6,0},{1,3},{3,5},{5,7},{7,1},{8,10},{10,12},{12... | collective-permute-start | bytes 1179656 | tf_op jit(solution)/shard_map/ppermute | solution.py:17
  31.2 28.5 %copy-start.2 = (bf16[2,32,64]{2,1,0:T(8,128)(2,1)S(1)}, bf16[2,32,64]{2,1,0:T(8,128)(2,1)}, u32[]{:S(2)}) copy-start(bf16[2,32,64]{2,1,0:T(8,128)(2,1)} %param.5) | copy-start | bytes 24580
  31.3 73.3 %collective-permute-start.4 = (bf16[256,3072]{1,0:T(8,128)(2,1)S(1)}, bf16[256,3072]{1,0:T(8,128)(2,1)}, u32[]{:S(2)}, u32[]{:S(2)}) collective-permute-start(bf16[256,3072]{1,0:T(8,128)(2,1)S(1)} %pad_maximum_fusion.a_mine), channel_id=1, source_target_pairs={{0,1},{1,0},{2,3},{3,2},{4,5},{5,4},{6,7},{7,6},{8,9},{9,8},{10,11... | collective-permute-start | bytes 4718600 | tf_op jit(solution)/shard_map/ppermute | solution.py:61
  33.2 23.0 %collective-permute-start.6 = (bf16[64,3072]{1,0:T(8,128)(2,1)S(1)}, bf16[64,3072]{1,0:T(8,128)(2,1)S(1)}, u32[]{:S(2)}, u32[]{:S(2)}) collective-permute-start(bf16[64,3072]{1,0:T(8,128)(2,1)S(1)} %collective-permute-done), channel_id=1, source_target_pairs={{0,6},{2,0},{4,2},{6,4},{1,7},{3,1},{5,3},{7,5},{8,14},{10,8},{12,... | collective-permute-start | bytes 1179656 | tf_op jit(solution)/shard_map/ppermute | solution.py:17
  35.9 21.1 %collective-permute-start.7 = (bf16[64,3072]{1,0:T(8,128)(2,1)S(1)}, bf16[64,3072]{1,0:T(8,128)(2,1)S(1)}, u32[]{:S(2)}, u32[]{:S(2)}) collective-permute-start(bf16[64,3072]{1,0:T(8,128)(2,1)S(1)} %collective-permute-done), channel_id=1, source_target_pairs={{0,4},{2,6},{4,0},{6,2},{1,5},{3,7},{5,1},{7,3},{8,12},{10,14},{12... | collective-permute-start | bytes 1179656 | tf_op jit(solution)/shard_map/ppermute | solution.py:17
  57.8 46.8 %collective-permute-start.8 = (bf16[256,3072]{1,0:T(8,128)(2,1)}, bf16[256,3072]{1,0:T(8,128)(2,1)}, u32[]{:S(2)}, u32[]{:S(2)}) collective-permute-start(bf16[256,3072]{1,0:T(8,128)(2,1)} %constant_dynamic-update-slice_fusion.b_mine), channel_id=1, source_target_pairs={{0,1},{1,0},{2,3},{3,2},{4,5},{5,4},{6,7},{7,6},{8,9},{9,8},{10,11... | collective-permute-start | bytes 4718600 | tf_op jit(solution)/shard_map/ppermute | solution.py:62
  59.7 7.0 %collective-permute-start.9 = (bf16[32,64]{1,0:T(8,128)(2,1)S(1)}, bf16[32,64]{1,0:T(8,128)(2,1)S(1)}, u32[]{:S(2)}, u32[]{:S(2)}) collective-permute-start(bf16[32,64]{1,0:T(8,128)(2,1)S(1)} %get-tuple-element.13), channel_id=1, source_target_pairs={{0,8},{8,0},{1,9},{9,1},{2,10},{10,2},{3,11},{11,3},{4,12},{12,4},... | collective-permute-start | bytes 12296 | tf_op jit(solution)/shard_map/ppermute | solution.py:50
  67.6 37.0 %all-to-all-start = ((bf16[32,32,128]{2,1,0:T(8,128)(2,1)}), bf16[32,32,128]{2,1,0:T(8,128)(2,1)S(1)}, u32[]{:S(2)}, u32[]{:S(2)}) async-start(bf16[32,32,128]{2,1,0:T(8,128)(2,1)} %broadcast_in_dim.65), calls=%async_computation | async-start | bytes 524288 | tf_op jit(solution)/shard_map/all_to_all | solution.py:59
  110.2 1.1 copy-start
  111.3 35.6 %all-to-all-start.1 = ((f32[32,32,128]{2,1,0:T(8,128)}), f32[32,32,128]{2,1,0:T(8,128)S(1)}, u32[]{:S(2)}, u32[]{:S(2)}) async-start(f32[32,32,128]{2,1,0:T(8,128)} %bitcast.13), calls=%async_computation.1 | async-start | bytes 1048576 | tf_op jit(solution)/shard_map/all_to_all | solution.py:87
  115.2 35.6 %copy-start.1 = (bf16[2,64,3072]{2,1,0:T(8,128)(2,1)S(1)}, bf16[2,64,3072]{2,1,0:T(8,128)(2,1)}, u32[]{:S(2)}) copy-start(bf16[2,64,3072]{2,1,0:T(8,128)(2,1)} %param.4) | copy-start | bytes 2359300
  116.8 34.0 %collective-permute-start.11 = (f32[64,3072]{1,0:T(8,128)S(1)}, f32[64,3072]{1,0:T(8,128)}, u32[]{:S(2)}, u32[]{:S(2)}) collective-permute-start(f32[64,3072]{1,0:T(8,128)S(1)} %get-tuple-element.7), channel_id=1, source_target_pairs={{0,8},{8,0},{1,9},{9,1},{2,10},{10,2},{3,11},{11,3},{4,12},{12,4},... | collective-permute-start | bytes 2359304 | tf_op jit(solution)/shard_map/ppermute | solution.py:82
  147.0 7.1 %collective-permute-start.10 = (f32[32,64]{1,0:T(8,128)S(1)}, f32[32,64]{1,0:T(8,128)S(1)}, u32[]{:S(2)}, u32[]{:S(2)}) collective-permute-start(f32[32,64]{1,0:T(8,128)S(1)} %get-tuple-element.11), channel_id=1, source_target_pairs={{0,8},{8,0},{1,9},{9,1},{2,10},{10,2},{3,11},{11,3},{4,12},{12,4},... | collective-permute-start | bytes 24584 | tf_op jit(solution)/shard_map/ppermute | solution.py:88

commit v2 on v0

v2 whole, which is shorter than its diff:
```python
import math

import jax
import jax.numpy as jnp
from jax import lax
from jax.experimental import pallas as pl
from jax.experimental.pallas import tpu as pltpu
from jax.sharding import Mesh, PartitionSpec as P

AXES = ("z", "yl", "yh", "x", "c")
ROW = ("z", "yl")
COL = ("yh", "x", "c")
SWAP = [(0, 1), (1, 0)]


def gram_products(index, mine, core, gram):
    width = gram.shape[2]
    runs = [pl.ds(pl.multiple_of((4 * yh + index[2]) * width, width), width) for yh in range(2)]
    own = jnp.concatenate([mine[run, :] for run in runs], axis=0)
    for rows, c in ((mine, index[1]), (core, 1 - index[1])):
        terms = lax.dot_general(rows[...], own, (((1,), (1,)), ((), ())), preferred_element_type=jnp.float32)
        gram[:, c] = terms.reshape(-1, width, 2 * width)


def recon_products(index, mine, core, h, h_yl, h_yh, h_both, keep, send):
    width = keep.shape[0]
    local = width // 2
    total = None
    for rows, c in ((mine, index[1]), (core, 1 - index[1])):
        picked = []
        for block in range(rows.shape[0] // width):
            at = pl.ds(pl.multiple_of((2 * block + c) * local, local), local)
            runs = []
            for ours, theirs in ((h, h_yh), (h_yl, h_both)):
                run = [jnp.where(index[0] == 0, part[at, :width], part[at, width:]) for part in (ours, theirs)]
                runs.append(jnp.concatenate(run, axis=1))
            picked.append(jnp.where(index[3] == 0, runs[0], runs[1]))
            picked.append(jnp.where(index[3] == 0, runs[1], runs[0]))
        factor = jnp.concatenate(picked, axis=0)
        term = lax.dot_general(factor, rows[...], (((0,), (0,)), ((), ())), preferred_element_type=jnp.float32)
        total = term if total is None else total + term
    send[...] = total[width:]
    keep[...] = total[:width]


def shards(slab_t, target_t, factor_h):
    yh, x, c = (lax.axis_index(name) for name in COL)
    yl = lax.axis_index("yl")
    width, rows = slab_t.shape[1:]
    nrow, nz, nx = lax.axis_size(ROW), lax.axis_size("z"), lax.axis_size("x")
    copies = jnp.broadcast_to(slab_t[:, None], (2, nx, width, rows)).reshape(2 * nx * width, rows)
    mine = lax.all_to_all(copies, ("yh", "x"), 0, 0, tiled=True)
    h_all = lax.all_gather(jnp.concatenate([factor_h[0], factor_h[1]], axis=1), "z", axis=0, tiled=True)
    h_yl = lax.ppermute(h_all, "yl", SWAP)
    h_yh = lax.ppermute(h_all, "yh", SWAP)
    h_both = lax.ppermute(h_all, ("yl", "yh"), [(i, 3 - i) for i in range(4)])
    mine, h_yl, h_yh, h_both = lax.optimization_barrier((mine, h_yl, h_yh, h_both))
    core = lax.ppermute(mine, "c", SWAP)

    index = jnp.stack([yh, c, x, yl]).astype(jnp.int32)
    smem, vmem = (pl.BlockSpec(memory_space=space) for space in (pltpu.SMEM, pltpu.VMEM))
    params = pltpu.CompilerParams(vmem_limit_bytes=40 * 2**20)
    cost = pl.CostEstimate(flops=2 * 16 * 2 * width * width * rows, bytes_accessed=8 * 2**20, transcendentals=0)
    half_like = jax.ShapeDtypeStruct((width, rows), jnp.float32)
    terms = pl.pallas_call(
        gram_products,
        out_shape=jax.ShapeDtypeStruct((2 * nx, 2, width, 2 * width), jnp.float32),
        in_specs=[smem] + [vmem] * 2,
        out_specs=vmem,
        compiler_params=params,
        cost_estimate=cost,
    )(index, mine, core)
    keep, send = pl.pallas_call(
        recon_products,
        out_shape=(half_like, half_like),
        in_specs=[smem] + [vmem] * 6,
        out_specs=(vmem,) * 2,
        compiler_params=params,
        cost_estimate=cost,
    )(index, mine, core, h_all, h_yl, h_yh, h_both)

    local = width // 2
    summed = lax.all_to_all(terms.reshape(nz, width, 2 * width), "z", 0, 0, tiled=True).sum(0)
    parts = summed.reshape(2, local, 2, width).transpose(0, 2, 1, 3).reshape(4, local, width)
    summed = lax.all_to_all(parts, ("yl", "yh"), 0, 0, tiled=True).reshape(2, 2, local, width).sum(0)

    slab = jnp.arange(2, dtype=jnp.int32)
    recon_other = lax.ppermute(send, "yh", SWAP)
    is_own = (slab == yh)[:, None, None]
    polar = target_t.astype(jnp.float32) - jnp.where(is_own, keep[None], recon_other[None])

    order_n = rows * nrow
    b_index = lax.axis_index(ROW) * local + jnp.arange(local, dtype=jnp.int32)
    a_index = lax.axis_index(COL) * width + jnp.arange(width, dtype=jnp.int32)
    identity = (b_index[:, None, None] == a_index[None, None, :]).astype(jnp.float32)
    gram = (summed.transpose(1, 0, 2) - order_n * identity) * (1.0 / math.sqrt(order_n))
    return (gram, polar)


def solution(mesh):
    parts = Mesh(mesh.devices.reshape(16, 2, 2, 4, 2), AXES)
    return jax.shard_map(
        shards,
        mesh=parts,
        in_specs=(P(None, COL, ROW), P(None, COL, ROW), P(None, ROW, COL)),
        out_specs=(P(ROW, None, COL), P(None, COL, ROW)),
        check_vma=False,
    )
```

time: 407 us -> 129 us (0.32)
  waiting for transfers between devices: 298 us -> 34.6 us
  blocking collectives: 73 us -> 34.1 us
  starting transfers between devices: 0.08 us -> 37.1 us
  matrix products: 16.8 us -> 0 us
  between operations: 14.7 us -> 0.82 us
  Pallas kernels: 0 us -> 7.72 us
  local copies, waits for them, and re-layouts: 2.54 us -> 8.49 us
    unnamed x3 -> x0, waiting for transfers between devices: 258 us -> none
    all_gather x1 -> x0, waiting for transfers between devices: 39.7 us -> none  [shards(): piece = lax.all_gather(slab_t, 'col', axis=1, tiled=True)]
    all_gather x1, blocking collectives: 73 us -> 34.1 us  [shards(): lax.all_gather(jnp.concatenate([factor_h[0], factor_h[1]], axis=1), 'z',...]
    all_to_all x0 -> x3, waiting for transfers between devices: none -> 23.3 us  [the longest x1 20.7 us: shards(): lax.all_to_all(terms.reshape(nz, width, 2 * width), 'z', 0, 0, tiled=True)]
    all_to_all x0 -> x3, starting transfers between devices: none -> 22.1 us  [the longest x1 9.55 us: shards(): mine = lax.all_to_all(copies, ('yh', 'x'), 0, 0, tiled=True)]
    dot_general x2 -> x0, matrix products: 16.8 us -> none  [the longest x1 8.75 us: shards(): jnp.einsum('sbn,san->bsa', piece, slab_t, preferred_element_type=jnp.floa...]
    ppermute x0 -> x5, starting transfers between devices: none -> 14.9 us  [the longest x1 5.48 us: shards(): h_yh = lax.ppermute(h_all, 'yh', SWAP)]
    ppermute x0 -> x5, waiting for transfers between devices: none -> 11.4 us  [the longest x1 5.67 us: shards(): core = lax.ppermute(mine, 'c', SWAP)]
  transfers between devices with their start and end apart: 2 -> 8, of which waited for: 2 -> 5; matrix products, arithmetic and copies ran while one was open for 2% -> 4% of each run, Pallas kernels for 0% -> 3%
where the time goes in v2:
time: 129 us; the launch traced here: 128 us
  starting transfers between devices  37.1 us (29%)
  waiting for transfers between devices  34.6 us (27%)
  blocking collectives  34.1 us (26%)
  local copies, waits for them, and re-layouts  8.49 us (7%)
  Pallas kernels  7.72 us (6%)
  other arithmetic  4.87 us (4%)
    all_gather x1, blocking collectives, shards(): lax.all_gather(jnp.concatenate([factor_h[0], factor_h[1]], axis=1), 'z',...  34.1 us
    all_to_all x1, waiting for transfers between devices, shards(): lax.all_to_all(terms.reshape(nz, width, 2 * width), 'z', 0, 0, tiled=True)  20.7 us
    all_to_all x1, starting transfers between devices, shards(): mine = lax.all_to_all(copies, ('yh', 'x'), 0, 0, tiled=True)  9.55 us
    all_to_all x1, starting transfers between devices, shards(): lax.all_to_all(terms.reshape(nz, width, 2 * width), 'z', 0, 0, tiled=True)  9.32 us
    ppermute x1, waiting for transfers between devices, shards(): core = lax.ppermute(mine, 'c', SWAP)  5.67 us
    ppermute x1, starting transfers between devices, shards(): h_yh = lax.ppermute(h_all, 'yh', SWAP)  5.48 us
    ppermute x1, waiting for transfers between devices, shards(): h_both = lax.ppermute(h_all, ('yl', 'yh'), [(i, 3 - i) for i in range(4)])  5.14 us
    unnamed x13, local copies, waits for them, and re-layouts  4.68 us
  transfers between devices with their start and end apart: 8, of which 5 were waited for; matrix products, arithmetic and copies ran while one was open for 4% of the time, Pallas kernels for 3%

profile of v2, /device:TPU:6, one launch (start us, length us, event | category | flops | bytes accessed | tf_op | source)
XLA Modules:
  0.0 127.7 jit_solution(14522729390487344069)
XLA Ops:
  0.6 3.2 %broadcast_in_dim.26 = bf16[2,4,64,3072]{3,2,1,0:T(8,128)(2,1)} broadcast(bf16[2,64,3072]{2,1,0:T(8,128)(2,1)} %param.3), dimensions={0,2,3} | broadcast | bytes 3932160 | tf_op jit(solution)/shard_map/broadcast_in_dim | solution.py:51
  3.8 0.0 copy-start.4
  3.8 9.5 %all-to-all-start = ((bf16[8,64,3072]{2,1,0:T(8,128)(2,1)}), bf16[8,64,3072]{2,1,0:T(8,128)(2,1)S(1)}, u32[]{:S(2)}, u32[]{:S(2)}) async-start(bf16[8,64,3072]{2,1,0:T(8,128)(2,1)} %bitcast.20), calls=%async_computation | async-start | bytes 6291456 | tf_op jit(solution)/shard_map/all_to_all | solution.py:52
  13.4 0.0 copy-done.4
  13.4 0.1 pad_maximum_fusion
  13.5 34.1 %all_gather.3.h = bf16[512,128]{1,0:T(8,128)(2,1)S(1)} all-gather(bf16[32,128]{1,0:T(8,128)(2,1)S(1)} %pad_maximum_fusion), channel_id=1, replica_groups=mesh['z'=16,'yl'=2,'yh'=2,'x'=4,'c'=2] {'z'}, dimensions={0}, use_global_device_ids=true | all-gather | bytes 139264 | tf_op jit(solution)/shard_map/all_gather | solution.py:53
  47.5 2.6 %collective-permute-start = (bf16[512,128]{1,0:T(8,128)(2,1)S(1)}, bf16[512,128]{1,0:T(8,128)(2,1)S(1)}, u32[]{:S(2)}, u32[]{:S(2)}) collective-permute-start(bf16[512,128]{1,0:T(8,128)(2,1)S(1)} %all_gather.3.h), channel_id=1, source_target_pairs={{0,16},{16,0},{1,17},{17,1},{2,18},{18,2},{3,19},{19,3},{4,20},{20... | collective-permute-start | bytes 393224 | tf_op jit(solution)/shard_map/ppermute | solution.py:54
  50.1 5.5 %collective-permute-start.1 = (bf16[512,128]{1,0:T(8,128)(2,1)S(1)}, bf16[512,128]{1,0:T(8,128)(2,1)S(1)}, u32[]{:S(2)}, u32[]{:S(2)}) collective-permute-start(bf16[512,128]{1,0:T(8,128)(2,1)S(1)} %all_gather.3.h), channel_id=1, source_target_pairs={{0,8},{8,0},{1,9},{9,1},{2,10},{10,2},{3,11},{11,3},{4,12},{12,4},... | collective-permute-start | bytes 393224 | tf_op jit(solution)/shard_map/ppermute | solution.py:55
  55.6 2.4 %collective-permute-start.2 = (bf16[512,128]{1,0:T(8,128)(2,1)S(1)}, bf16[512,128]{1,0:T(8,128)(2,1)S(1)}, u32[]{:S(2)}, u32[]{:S(2)}) collective-permute-start(bf16[512,128]{1,0:T(8,128)(2,1)S(1)} %all_gather.3.h), channel_id=1, source_target_pairs={{0,24},{8,16},{16,8},{24,0},{1,25},{9,17},{17,9},{25,1},{2,26},{10... | collective-permute-start | bytes 393224 | tf_op jit(solution)/shard_map/ppermute | solution.py:56
  58.0 0.0 collective-permute-done.h_yl
  58.0 0.6 collective-permute-done.1.h_yh
  58.5 5.1 %collective-permute-done.2.h_both = bf16[512,128]{1,0:T(8,128)(2,1)S(1)} collective-permute-done((bf16[512,128]{1,0:T(8,128)(2,1)S(1)}, bf16[512,128]{1,0:T(8,128)(2,1)S(1)}, u32[]{:S(2)}, u32[]{:S(2)}) %collective-permute-start.2) | collective-permute-done | bytes 131104 | tf_op jit(solution)/shard_map/ppermute | solution.py:56
  63.7 0.0 copy-start.2
  63.7 0.7 copy-done.2
  64.3 0.0 all-to-all-done
  64.3 1.9 %collective-permute-start.3 = (bf16[512,3072]{1,0:T(8,128)(2,1)S(1)}, bf16[512,3072]{1,0:T(8,128)(2,1)}, u32[]{:S(2)}, u32[]{:S(2)}) collective-permute-start(bf16[512,3072]{1,0:T(8,128)(2,1)S(1)} %bitcast.16), channel_id=1, source_target_pairs={{0,1},{1,0},{2,3},{3,2},{4,5},{5,4},{6,7},{7,6},{8,9},{9,8},{10,11... | collective-permute-start | bytes 9437192 | tf_op jit(solution)/shard_map/ppermute | solution.py:58
  66.3 0.1 pad_add_fusion.index
  66.3 5.7 %collective-permute-done.3.core = bf16[512,3072]{1,0:T(8,128)(2,1)} collective-permute-done((bf16[512,3072]{1,0:T(8,128)(2,1)S(1)}, bf16[512,3072]{1,0:T(8,128)(2,1)}, u32[]{:S(2)}, u32[]{:S(2)}) %collective-permute-start.3) | collective-permute-done | bytes 3145760 | tf_op jit(solution)/shard_map/ppermute | solution.py:58
  72.0 3.7 %shard_map.50 = f32[8,2,64,128]{3,2,1,0:T(8,128)S(1)} custom-call(s32[4]{0:T(128)S(1)} %pad_add_fusion.index, bf16[512,3072]{1,0:T(8,128)(2,1)S(1)} %bitcast.17, bf16[512,3072]{1,0:T(8,128)(2,1)} %collective-permute-done.3.core), custom_call_target="tpu_custom_call" | custom-call | flops 805306368 | bytes 8388608 | tf_op jit(solution)/shard_map/pallas_call | solution.py:65
  75.7 0.0 copy-start
  75.7 0.8 copy-done
  76.5 9.3 %all-to-all-start.1 = ((f32[16,64,128]{2,1,0:T(8,128)}), f32[16,64,128]{2,1,0:T(8,128)}, u32[]{:S(2)}, u32[]{:S(2)}) async-start(f32[16,64,128]{2,1,0:T(8,128)} %bitcast.19), calls=%async_computation.1 | async-start | bytes 1048576 | tf_op jit(solution)/shard_map/all_to_all | solution.py:83
  85.8 0.0 copy-start.3
  85.8 0.9 copy-done.3
  86.7 4.0 %shard_map.51 = (f32[64,3072]{1,0:T(8,128)S(1)}, f32[64,3072]{1,0:T(8,128)}) custom-call(s32[4]{0:T(128)S(1)} %pad_add_fusion.index, bf16[512,3072]{1,0:T(8,128)(2,1)S(1)} %bitcast.18, bf16[512,3072]{1,0:T(8,128)(2,1)} %collective-permute-done.3.core, bf16[512,128]{1,0:T(8,128)(2,1)S(1)} %all_gather.3.h, bf16[512,128]{1,0:T(8,128)(2,1)S(1)} %collective-permute-done.h_yl, ...), custom_call_target="tpu_custom_call" | custom-call | flops 805306368 | bytes 8388608 | tf_op jit(solution)/shard_map/pallas_call | solution.py:73
  90.8 0.0 copy-start.1
  90.8 0.9 copy-done.1
  91.6 2.6 %collective-permute-start.4 = (f32[64,3072]{1,0:T(8,128)}, f32[64,3072]{1,0:T(8,128)S(1)}, u32[]{:S(2)}, u32[]{:S(2)}) collective-permute-start(f32[64,3072]{1,0:T(8,128)} %get-tuple-element.13), channel_id=1, source_target_pairs={{0,8},{8,0},{1,9},{9,1},{2,10},{10,2},{3,11},{11,3},{4,12},{12,4},... | collective-permute-start | bytes 2359304 | tf_op jit(solution)/shard_map/ppermute | solution.py:88
  94.3 0.1 compare_select_fusion
  94.4 20.7 %all-to-all-done.1 = f32[16,64,128]{2,1,0:T(8,128)} async-done(((f32[16,64,128]{2,1,0:T(8,128)}), f32[16,64,128]{2,1,0:T(8,128)}, u32[]{:S(2)}, u32[]{:S(2)}) %all-to-all-start.1) | async-done | bytes 524320 | tf_op jit(solution)/shard_map/all_to_all | solution.py:83
  115.1 1.1 reduce_sum.18
  116.2 0.1 reshape.68
  116.3 0.7 reshape.71
  117.0 3.3 %all-to-all-start.2 = ((f32[4,1,2048]{2,1,0:T(1,128)}), f32[4,1,2048]{2,1,0:T(1,128)S(1)}, u32[]{:S(2)}, u32[]{:S(2)}) async-start(f32[4,1,2048]{2,1,0:T(1,128)} %reshape.71), calls=%async_computation.2 | async-start | bytes 65536 | tf_op jit(solution)/shard_map/all_to_all | solution.py:85
  120.3 0.0 collective-permute-done.4
  120.3 2.8 %select_subtract_fusion = f32[2,64,3072]{2,1,0:T(8,128)} fusion(bf16[2,64,3072]{2,1,0:T(8,128)(2,1)} %param.4, f32[64,3072]{1,0:T(8,128)S(1)} %collective-permute-done.4, f32[64,3072]{1,0:T(8,128)} %copy-done.1, pred[2]{0:T(512)(128)(4,1)S(1)} %iota_compare_fusion), kind=kLoop, calls=%fused_computation | loop fusion | flops 1179648 | bytes 3932162 | tf_op jit(solution)/shard_map/sub | solution.py:90
  123.1 2.5 %all-to-all-done.2 = f32[4,1,2048]{2,1,0:T(1,128)S(1)} async-done(((f32[4,1,2048]{2,1,0:T(1,128)}), f32[4,1,2048]{2,1,0:T(1,128)S(1)}, u32[]{:S(2)}, u32[]{:S(2)}) %all-to-all-start.2) | async-done | bytes 32800 | tf_op jit(solution)/shard_map/all_to_all | solution.py:85
  125.6 0.5 broadcast.51
  126.2 0.7 reduce
  126.9 0.1 reshape.72
  127.0 0.6 copy.7
  (7 shorter events, 0.0 us)
Async XLA Ops:
  3.8 9.6 %copy-start.4 = (bf16[2,32,64]{2,1,0:T(8,128)(2,1)S(1)}, bf16[2,32,64]{2,1,0:T(8,128)(2,1)}, u32[]{:S(2)}) copy-start(bf16[2,32,64]{2,1,0:T(8,128)(2,1)} %param.5) | copy-start | bytes 24580
  3.8 60.5 %all-to-all-start = ((bf16[8,64,3072]{2,1,0:T(8,128)(2,1)}), bf16[8,64,3072]{2,1,0:T(8,128)(2,1)S(1)}, u32[]{:S(2)}, u32[]{:S(2)}) async-start(bf16[8,64,3072]{2,1,0:T(8,128)(2,1)} %bitcast.20), calls=%async_computation | async-start | bytes 6291456 | tf_op jit(solution)/shard_map/all_to_all | solution.py:52
  47.5 10.4 %collective-permute-start = (bf16[512,128]{1,0:T(8,128)(2,1)S(1)}, bf16[512,128]{1,0:T(8,128)(2,1)S(1)}, u32[]{:S(2)}, u32[]{:S(2)}) collective-permute-start(bf16[512,128]{1,0:T(8,128)(2,1)S(1)} %all_gather.3.h), channel_id=1, source_target_pairs={{0,16},{16,0},{1,17},{17,1},{2,18},{18,2},{3,19},{19,3},{4,20},{20... | collective-permute-start | bytes 393224 | tf_op jit(solution)/shard_map/ppermute | solution.py:54
  50.1 8.4 %collective-permute-start.1 = (bf16[512,128]{1,0:T(8,128)(2,1)S(1)}, bf16[512,128]{1,0:T(8,128)(2,1)S(1)}, u32[]{:S(2)}, u32[]{:S(2)}) collective-permute-start(bf16[512,128]{1,0:T(8,128)(2,1)S(1)} %all_gather.3.h), channel_id=1, source_target_pairs={{0,8},{8,0},{1,9},{9,1},{2,10},{10,2},{3,11},{11,3},{4,12},{12,4},... | collective-permute-start | bytes 393224 | tf_op jit(solution)/shard_map/ppermute | solution.py:55
  55.6 8.1 %collective-permute-start.2 = (bf16[512,128]{1,0:T(8,128)(2,1)S(1)}, bf16[512,128]{1,0:T(8,128)(2,1)S(1)}, u32[]{:S(2)}, u32[]{:S(2)}) collective-permute-start(bf16[512,128]{1,0:T(8,128)(2,1)S(1)} %all_gather.3.h), channel_id=1, source_target_pairs={{0,24},{8,16},{16,8},{24,0},{1,25},{9,17},{17,9},{25,1},{2,26},{10... | collective-permute-start | bytes 393224 | tf_op jit(solution)/shard_map/ppermute | solution.py:56
  63.7 0.7 copy-start.2
  64.3 7.7 %collective-permute-start.3 = (bf16[512,3072]{1,0:T(8,128)(2,1)S(1)}, bf16[512,3072]{1,0:T(8,128)(2,1)}, u32[]{:S(2)}, u32[]{:S(2)}) collective-permute-start(bf16[512,3072]{1,0:T(8,128)(2,1)S(1)} %bitcast.16), channel_id=1, source_target_pairs={{0,1},{1,0},{2,3},{3,2},{4,5},{5,4},{6,7},{7,6},{8,9},{9,8},{10,11... | collective-permute-start | bytes 9437192 | tf_op jit(solution)/shard_map/ppermute | solution.py:58
  75.7 0.8 copy-start
  76.5 38.6 %all-to-all-start.1 = ((f32[16,64,128]{2,1,0:T(8,128)}), f32[16,64,128]{2,1,0:T(8,128)}, u32[]{:S(2)}, u32[]{:S(2)}) async-start(f32[16,64,128]{2,1,0:T(8,128)} %bitcast.19), calls=%async_computation.1 | async-start | bytes 1048576 | tf_op jit(solution)/shard_map/all_to_all | solution.py:83
  85.8 0.9 copy-start.3
  90.8 0.9 copy-start.1
  91.6 28.7 %collective-permute-start.4 = (f32[64,3072]{1,0:T(8,128)}, f32[64,3072]{1,0:T(8,128)S(1)}, u32[]{:S(2)}, u32[]{:S(2)}) collective-permute-start(f32[64,3072]{1,0:T(8,128)} %get-tuple-element.13), channel_id=1, source_target_pairs={{0,8},{8,0},{1,9},{9,1},{2,10},{10,2},{3,11},{11,3},{4,12},{12,4},... | collective-permute-start | bytes 2359304 | tf_op jit(solution)/shard_map/ppermute | solution.py:88
  117.0 8.6 %all-to-all-start.2 = ((f32[4,1,2048]{2,1,0:T(1,128)}), f32[4,1,2048]{2,1,0:T(1,128)S(1)}, u32[]{:S(2)}, u32[]{:S(2)}) async-start(f32[4,1,2048]{2,1,0:T(1,128)} %reshape.71), calls=%async_computation.2 | async-start | bytes 65536 | tf_op jit(solution)/shard_map/all_to_all | solution.py:85

commit v3 on v2

v3 whole, which is shorter than its diff:
```python
import functools
import itertools
import math

import jax
import jax.numpy as jnp
from jax import lax
from jax.experimental import pallas as pl
from jax.experimental.pallas import tpu as pltpu
from jax.sharding import Mesh, PartitionSpec as P

AXES = ("z", "yl", "yh", "x", "c")
ROW = ("z", "yl")
COL = ("yh", "x", "c")
SWAP = [(0, 1), (1, 0)]


def spread(slab, copies, sems):
    half = copies.shape[4]
    started = []
    for yh, x, c in itertools.product(*map(range, copies.shape[:3])):
        source = slab.at[yh, :, pl.ds(c * half, half)]
        started.append(pltpu.make_async_copy(source, copies.at[yh, x, c], sems.at[len(started)]))
        started[-1].start()
    for copy in started:
        copy.wait()


def gram_products(index, mine, core):
    width = mine.shape[0] // 16
    c = index[1] if core == 0 else 1 - index[1]
    own = [mine[pl.ds(pl.multiple_of((8 * yh + 2 * index[2] + c) * width, width), width), :] for yh in range(2)]
    own = jnp.concatenate(own, axis=0)
    terms = lax.dot_general(mine[...], own, (((1,), (1,)), ((), ())), preferred_element_type=jnp.float32)
    terms = terms.reshape(-1, 2, 2, width // 4, 2 * width)
    parts = []
    for yh in range(2):
        columns = terms[..., yh * width:(yh + 1) * width]
        parts.append(jnp.concatenate([columns[:, :, 0], columns[:, :, 1]], axis=-1))
    return parts


def other_core_gram(index, mine, gram):
    for yh, part in enumerate(gram_products(index, mine, 1)):
        gram[:, :, yh] = part


def this_core_gram(index, mine, received, keep, send):
    for yh, part in enumerate(gram_products(index, mine, 0)):
        total = part + received[:, :, yh]
        keep[:, yh] = jnp.where(index[3] == 0, total[:, 0], total[:, 1])
        send[:, yh] = jnp.where(index[3] == 0, total[:, 1], total[:, 0])


def arrange(index, h, h_yl, h_yh, h_both, factor):
    width = factor.shape[1] // 2
    halves = []
    for parts in ((h, h_yh), (h_yl, h_both)):
        runs = [jnp.where(index[0] == 0, part[:, :width], part[:, width:]) for part in parts]
        halves.append(jnp.concatenate(runs, axis=1))
    pair = [jnp.where(index[3] == yl, halves[0], halves[1]).reshape(-1, width // 2, 2 * width) for yl in range(2)]
    factor[...] = jnp.stack(pair, axis=1).reshape(factor.shape)


def recon_products(index, mine, core, factor, keep, send):
    width, half = keep.shape[0], mine.shape[1]
    for rows, c in ((mine, index[1]), (core, 1 - index[1])):
        total = lax.dot_general(factor[...], rows[...], (((0,), (0,)), ((), ())), preferred_element_type=jnp.float32)
        at = pl.ds(pl.multiple_of(c * half, half), half)
        send[:, at] = total[width:]
        keep[:, at] = total[:width]


def shards(slab_t, target_t, factor_h):
    yh, x, c = (lax.axis_index(name) for name in COL)
    yl = lax.axis_index("yl")
    width, rows = slab_t.shape[1:]
    nrow, nz, nx = lax.axis_size(ROW), lax.axis_size("z"), lax.axis_size("x")
    half = rows // 2
    smem, vmem, anywhere = (pl.BlockSpec(memory_space=space) for space in (pltpu.SMEM, pltpu.VMEM, pl.ANY))
    copies = pl.pallas_call(
        spread,
        out_shape=jax.ShapeDtypeStruct((2, nx, 2, width, half), slab_t.dtype),
        in_specs=[vmem],
        out_specs=anywhere,
        scratch_shapes=[pltpu.SemaphoreType.DMA((4 * nx,))],
    )(slab_t)
    mine = lax.all_to_all(copies.reshape(4 * nx, width, half), COL, 0, 0).reshape(4 * nx * width, half)
    h_all = lax.all_gather(jnp.concatenate([factor_h[0], factor_h[1]], axis=1), "z", axis=0, tiled=True)
    h_yl = lax.ppermute(h_all, "yl", SWAP)
    h_yh = lax.ppermute(h_all, "yh", SWAP)
    h_both = lax.ppermute(h_all, ("yl", "yh"), [(i, 3 - i) for i in range(4)])
    mine, h_yl, h_yh, h_both = lax.optimization_barrier((mine, h_yl, h_yh, h_both))

    index = jnp.stack([yh, c, x, yl]).astype(jnp.int32)
    params = pltpu.CompilerParams(vmem_limit_bytes=14 * 2**20)
    half_like = jax.ShapeDtypeStruct((width, rows), jnp.float32)
    cost = pl.CostEstimate(flops=2 * 16 * 2 * width * width * rows, bytes_accessed=8 * 2**20, transcendentals=0)

    gram_like = jax.ShapeDtypeStruct((nz, 2, 2, width // 4, 2 * width), jnp.float32)
    row_like = jax.ShapeDtypeStruct((nz, 2, width // 4, 2 * width), jnp.float32)
    core_terms = pl.pallas_call(
        other_core_gram,
        out_shape=gram_like,
        in_specs=[smem, vmem],
        out_specs=vmem,
        compiler_params=params,
        cost_estimate=cost,
    )(index, mine)
    core = lax.ppermute(mine, "c", SWAP)
    core_terms = lax.ppermute(core_terms, "c", SWAP)
    factor = pl.pallas_call(
        arrange,
        out_shape=jax.ShapeDtypeStruct((4 * nx * width, 2 * width), slab_t.dtype),
        in_specs=[smem] + [vmem] * 4,
        out_specs=vmem,
        compiler_params=params,
        cost_estimate=pl.CostEstimate(flops=0, bytes_accessed=2**20, transcendentals=0),
    )(index, h_all, h_yl, h_yh, h_both)
    terms, yl_terms = pl.pallas_call(
        this_core_gram,
        out_shape=(row_like, row_like),
        in_specs=[smem, vmem, vmem],
        out_specs=(vmem, vmem),
        compiler_params=params,
        cost_estimate=cost,
    )(index, mine, core_terms)
    yl_terms = lax.ppermute(yl_terms, "yl", SWAP)
    keep, send = pl.pallas_call(
        recon_products,
        out_shape=(half_like, half_like),
        in_specs=[smem] + [vmem] * 3,
        out_specs=(vmem,) * 2,
        compiler_params=params,
        cost_estimate=cost,
    )(index, mine, core, factor)
    terms, yl_terms, send = lax.optimization_barrier((terms, yl_terms, send))
    recon_other = lax.ppermute(send, "yh", SWAP)
    terms = terms + yl_terms
    local = width // 2
    parts = lax.all_to_all(terms.reshape(nrow, width // 4, 2 * width), ("z", "yh"), 0, 0)
    summed = parts.reshape(nz, 2, width // 4, 2, width).sum(0).transpose(2, 1, 0, 3).reshape(local, 2, width)

    slab = jnp.arange(2, dtype=jnp.int32)
    is_own = (slab == yh)[:, None, None]
    polar = target_t.astype(jnp.float32) - jnp.where(is_own, keep[None], recon_other[None])

    order_n = rows * nrow
    b_index = lax.axis_index(ROW) * local + jnp.arange(local, dtype=jnp.int32)
    a_index = lax.axis_index(COL) * width + jnp.arange(width, dtype=jnp.int32)
    identity = (b_index[:, None, None] == a_index[None, None, :]).astype(jnp.float32)
    gram = (summed - order_n * identity) * (1.0 / math.sqrt(order_n))
    return (gram, polar)


def solution(mesh):
    parts = Mesh(mesh.devices.reshape(16, 2, 2, 4, 2), AXES)
    return jax.shard_map(
        shards,
        mesh=parts,
        in_specs=(P(None, COL, ROW), P(None, COL, ROW), P(None, ROW, COL)),
        out_specs=(P(ROW, None, COL), P(None, COL, ROW)),
        check_vma=False,
    )
```

time: 129 us -> 124 us (0.961)
  waiting for transfers between devices: 34.6 us -> 27.5 us
  local copies, waits for them, and re-layouts: 8.49 us -> 4.49 us
  Pallas kernels: 7.72 us -> 10.9 us
  starting transfers between devices: 37.1 us -> 39.6 us
    all_to_all x3 -> x2, waiting for transfers between devices: 23.3 us -> 10.6 us  [the longest x1 10.6 us: shards(): lax.all_to_all(terms.reshape(nrow, width // 4, 2 * width), ('z', 'yh'), 0...]
    ppermute x1, waiting for transfers between devices: 0.01 us -> 7.81 us  [shards(): recon_other = lax.ppermute(send, 'yh', SWAP)]
    ppermute x1, waiting for transfers between devices: 5.67 us -> 0.01 us  [shards(): core = lax.ppermute(mine, 'c', SWAP)]
    ppermute x0 -> x2, waiting for transfers between devices: none -> 4.65 us  [the longest x1 2.54 us: shards(): yl_terms = lax.ppermute(yl_terms, 'yl', SWAP)]
    ppermute x0 -> x2, starting transfers between devices: none -> 4.47 us  [the longest x1 2.55 us: shards(): core_terms = lax.ppermute(core_terms, 'c', SWAP)]
    pallas_call x1 -> x4, Pallas kernels: 3.7 us -> 7.12 us  [the longest x1 2.93 us: shards(): pl.pallas_call(spread, out_shape=jax.ShapeDtypeStruct((2, nx, 2, width, h...]
    broadcast_in_dim x1 -> x0, local copies, waits for them, and re-layouts: 3.19 us -> none  [shards(): jnp.broadcast_to(slab_t[:, None], (2, nx, width, rows))]
    add x0 -> x1, other arithmetic: none -> 1.69 us  [shards(): terms = terms + yl_terms]
  transfers between devices with their start and end apart: 8 -> 9, of which waited for: 5 -> 5; matrix products, arithmetic and copies ran while one was open for 4% -> 4% of each run, Pallas kernels for 3% -> 7%
where the time goes in v3:
time: 124 us; the launch traced here: 122 us
  starting transfers between devices  39.6 us (32%)
  blocking collectives  34.1 us (28%)
  waiting for transfers between devices  27.5 us (22%)
  Pallas kernels  10.9 us (9%)
  other arithmetic  4.72 us (4%)
  local copies, waits for them, and re-layouts  4.49 us (4%)
    all_gather x1, blocking collectives, shards(): lax.all_gather(jnp.concatenate([factor_h[0], factor_h[1]], axis=1), 'z',...  34.1 us
    all_to_all x1, starting transfers between devices, shards(): lax.all_to_all(terms.reshape(nrow, width // 4, 2 * width), ('z', 'yh'), 0...  11.3 us
    all_to_all x1, waiting for transfers between devices, shards(): lax.all_to_all(terms.reshape(nrow, width // 4, 2 * width), ('z', 'yh'), 0...  10.6 us
    all_to_all x1, starting transfers between devices, shards(): lax.all_to_all(copies.reshape(4 * nx, width, half), COL, 0, 0)  9.43 us
    ppermute x1, waiting for transfers between devices, shards(): recon_other = lax.ppermute(send, 'yh', SWAP)  7.81 us
    ppermute x1, starting transfers between devices, shards(): h_yh = lax.ppermute(h_all, 'yh', SWAP)  5.48 us
    ppermute x1, waiting for transfers between devices, shards(): h_both = lax.ppermute(h_all, ('yl', 'yh'), [(i, 3 - i) for i in range(4)])  4.4 us
    unnamed x21, local copies, waits for them, and re-layouts  4.16 us
  transfers between devices with their start and end apart: 9, of which 5 were waited for; matrix products, arithmetic and copies ran while one was open for 4% of the time, Pallas kernels for 7%

profile of v3, /device:TPU:6, one launch (start us, length us, event | category | flops | bytes accessed | tf_op | source)
XLA Modules:
  0.0 122.2 jit_solution(4052865413018261392)
XLA Ops:
  0.6 2.9 %shard_map.50 = bf16[2,4,2,64,1536]{4,3,2,1,0:T(8,128)(2,1)} custom-call(bf16[2,64,3072]{2,1,0:T(8,128)(2,1)} %slab.1), custom_call_target="tpu_custom_call" | custom-call | tf_op jit(solution)/shard_map/pallas_call | solution.py:81
  3.6 0.0 copy-start.9
  3.6 9.4 %all-to-all-start = ((bf16[16,64,1536]{2,1,0:T(8,128)(2,1)}), bf16[16,64,1536]{2,1,0:T(8,128)(2,1)S(1)}, u32[]{:S(2)}, u32[]{:S(2)}) async-start(bf16[16,64,1536]{2,1,0:T(8,128)(2,1)} %bitcast.20), calls=%async_computation | async-start | bytes 6291456 | tf_op jit(solution)/shard_map/all_to_all | solution.py:88
  13.0 0.0 copy-done.9
  13.0 0.1 pad_maximum_fusion
  13.1 34.1 %all_gather.3.h = bf16[512,128]{1,0:T(8,128)(2,1)S(1)} all-gather(bf16[32,128]{1,0:T(8,128)(2,1)S(1)} %pad_maximum_fusion), channel_id=1, replica_groups=mesh['z'=16,'yl'=2,'yh'=2,'x'=4,'c'=2] {'z'}, dimensions={0}, use_global_device_ids=true | all-gather | bytes 139264 | tf_op jit(solution)/shard_map/all_gather | solution.py:89
  47.2 2.6 %collective-permute-start = (bf16[512,128]{1,0:T(8,128)(2,1)S(1)}, bf16[512,128]{1,0:T(8,128)(2,1)S(1)}, u32[]{:S(2)}, u32[]{:S(2)}) collective-permute-start(bf16[512,128]{1,0:T(8,128)(2,1)S(1)} %all_gather.3.h), channel_id=1, source_target_pairs={{0,16},{16,0},{1,17},{17,1},{2,18},{18,2},{3,19},{19,3},{4,20},{20... | collective-permute-start | bytes 393224 | tf_op jit(solution)/shard_map/ppermute | solution.py:90
  49.8 5.5 %collective-permute-start.1 = (bf16[512,128]{1,0:T(8,128)(2,1)S(1)}, bf16[512,128]{1,0:T(8,128)(2,1)S(1)}, u32[]{:S(2)}, u32[]{:S(2)}) collective-permute-start(bf16[512,128]{1,0:T(8,128)(2,1)S(1)} %all_gather.3.h), channel_id=1, source_target_pairs={{0,8},{8,0},{1,9},{9,1},{2,10},{10,2},{3,11},{11,3},{4,12},{12,4},... | collective-permute-start | bytes 393224 | tf_op jit(solution)/shard_map/ppermute | solution.py:91
  55.3 2.4 %collective-permute-start.2 = (bf16[512,128]{1,0:T(8,128)(2,1)S(1)}, bf16[512,128]{1,0:T(8,128)(2,1)S(1)}, u32[]{:S(2)}, u32[]{:S(2)}) collective-permute-start(bf16[512,128]{1,0:T(8,128)(2,1)S(1)} %all_gather.3.h), channel_id=1, source_target_pairs={{0,24},{8,16},{16,8},{24,0},{1,25},{9,17},{17,9},{25,1},{2,26},{10... | collective-permute-start | bytes 393224 | tf_op jit(solution)/shard_map/ppermute | solution.py:92
  57.6 0.0 collective-permute-done.h_yl
  57.6 0.0 copy-start.2
  57.6 0.6 copy-done.2
  58.3 0.0 collective-permute-done.1.h_yh
  58.3 0.0 copy-start.4
  58.3 0.6 copy-done.4
  58.9 4.4 %collective-permute-done.2.h_both = bf16[512,128]{1,0:T(8,128)(2,1)S(1)} collective-permute-done((bf16[512,128]{1,0:T(8,128)(2,1)S(1)}, bf16[512,128]{1,0:T(8,128)(2,1)S(1)}, u32[]{:S(2)}, u32[]{:S(2)}) %collective-permute-start.2) | collective-permute-done | bytes 131104 | tf_op jit(solution)/shard_map/ppermute | solution.py:92
  63.3 0.6 copy-done.6
  64.0 0.0 all-to-all-done
  64.0 1.9 %collective-permute-start.5 = (bf16[1024,1536]{1,0:T(8,128)(2,1)S(1)}, bf16[1024,1536]{1,0:T(8,128)(2,1)}, u32[]{:S(2)}, u32[]{:S(2)}) collective-permute-start(bf16[1024,1536]{1,0:T(8,128)(2,1)S(1)} %bitcast.16), channel_id=1, source_target_pairs={{0,1},{1,0},{2,3},{3,2},{4,5},{5,4},{6,7},{7,6},{8,9},{9,8},{10,11... | collective-permute-start | bytes 9437192 | tf_op jit(solution)/shard_map/ppermute | solution.py:110
  65.9 0.1 pad_add_fusion.index
  66.0 1.6 %shard_map.51 = f32[16,2,2,16,128]{4,3,2,1,0:T(8,128)S(1)} custom-call(s32[4]{0:T(128)S(1)} %pad_add_fusion.index, bf16[1024,1536]{1,0:T(8,128)(2,1)S(1)} %bitcast.17), custom_call_target="tpu_custom_call" | custom-call | flops 805306368 | bytes 8388608 | tf_op jit(solution)/shard_map/pallas_call | solution.py:102
  67.6 0.0 copy-start.3
  67.6 0.0 copy-start.5
  67.6 0.0 copy-start.7
  67.6 2.5 %collective-permute-start.3 = (f32[16,2,2,16,128]{4,3,2,1,0:T(8,128)S(1)}, f32[16,2,2,16,128]{4,3,2,1,0:T(8,128)S(1)}, u32[]{:S(2)}, u32[]{:S(2)}) collective-permute-start(f32[16,2,2,16,128]{4,3,2,1,0:T(8,128)S(1)} %shard_map.51), channel_id=1, source_target_pairs={{0,1},{1,0},{2,3},{3,2},{4,5},{5,4},{6,7},{7,6},{8,9},{9,8},{10,11... | collective-permute-start | bytes 1572872 | tf_op jit(solution)/shard_map/ppermute | solution.py:111
  70.2 2.1 %collective-permute-done.3.received = f32[16,2,2,16,128]{4,3,2,1,0:T(8,128)S(1)} collective-permute-done((f32[16,2,2,16,128]{4,3,2,1,0:T(8,128)S(1)}, f32[16,2,2,16,128]{4,3,2,1,0:T(8,128)S(1)}, u32[]{:S(2)}, u32[]{:S(2)}) %collective-permute-start.3) | collective-permute-done | bytes 524320 | tf_op jit(solution)/shard_map/ppermute | solution.py:111
  72.3 1.6 %shard_map.52 = (f32[16,2,16,128]{3,2,1,0:T(8,128)S(1)}, f32[16,2,16,128]{3,2,1,0:T(8,128)S(1)}) custom-call(s32[4]{0:T(128)S(1)} %pad_add_fusion.index, bf16[1024,1536]{1,0:T(8,128)(2,1)S(1)} %bitcast.18, f32[16,2,2,16,128]{4,3,2,1,0:T(8,128)S(1)} %collective-permute-done.3.received), custom_call_target="tpu_custom_call" | custom-call | flops 805306368 | bytes 8388608 | tf_op jit(solution)/shard_map/pallas_call | solution.py:120
  73.9 1.9 %collective-permute-start.4 = (f32[16,2,16,128]{3,2,1,0:T(8,128)S(1)}, f32[16,2,16,128]{3,2,1,0:T(8,128)S(1)}, u32[]{:S(2)}, u32[]{:S(2)}) collective-permute-start(f32[16,2,16,128]{3,2,1,0:T(8,128)S(1)} %get-tuple-element.15), channel_id=1, source_target_pairs={{0,16},{16,0},{1,17},{17,1},{2,18},{18,2},{3,19},{19,3},{4,20},{20... | collective-permute-start | bytes 786440 | tf_op jit(solution)/shard_map/ppermute | solution.py:128
  75.8 0.0 copy-done.3
  75.8 0.0 copy-done.5
  75.8 0.0 copy-done.7
  75.8 1.0 shard_map.53.factor
  76.8 0.0 collective-permute-done.5.core
  76.9 3.8 %shard_map.54 = (f32[64,3072]{1,0:T(8,128)S(1)}, f32[64,3072]{1,0:T(8,128)}) custom-call(s32[4]{0:T(128)S(1)} %pad_add_fusion.index, bf16[1024,1536]{1,0:T(8,128)(2,1)S(1)} %bitcast.19, bf16[1024,1536]{1,0:T(8,128)(2,1)} %collective-permute-done.5.core, bf16[1024,128]{1,0:T(8,128)(2,1)S(1)} %shard_map.53.factor), custom_call_target="tpu_custom_call" | custom-call | flops 805306368 | bytes 8388608 | tf_op jit(solution)/shard_map/pallas_call | solution.py:129
  80.7 0.9 copy-done
  81.6 2.5 %collective-permute-done.4 = f32[16,2,16,128]{3,2,1,0:T(8,128)S(1)} collective-permute-done((f32[16,2,16,128]{3,2,1,0:T(8,128)S(1)}, f32[16,2,16,128]{3,2,1,0:T(8,128)S(1)}, u32[]{:S(2)}, u32[]{:S(2)}) %collective-permute-start.4) | collective-permute-done | bytes 262176 | tf_op jit(solution)/shard_map/ppermute | solution.py:128
  84.1 0.7 copy-done.8
  84.8 2.1 %collective-permute-start.6 = (f32[64,3072]{1,0:T(8,128)}, f32[64,3072]{1,0:T(8,128)S(1)}, u32[]{:S(2)}, u32[]{:S(2)}) collective-permute-start(f32[64,3072]{1,0:T(8,128)} %get-tuple-element.23), channel_id=1, source_target_pairs={{0,8},{8,0},{1,9},{9,1},{2,10},{10,2},{3,11},{11,3},{4,12},{12,4},... | collective-permute-start | bytes 2359304 | tf_op jit(solution)/shard_map/ppermute | solution.py:138
  86.9 1.7 %add.32 = f32[16,2,16,128]{3,2,1,0:T(8,128)} add(f32[16,2,16,128]{3,2,1,0:T(8,128)S(1)} %get-tuple-element.20, f32[16,2,16,128]{3,2,1,0:T(8,128)} %copy-done.8) | non-fusion elementwise | flops 65536 | bytes 786432 | tf_op jit(solution)/shard_map/add | solution.py:139
  88.6 11.3 %all-to-all-start.1 = ((f32[32,16,128]{2,1,0:T(8,128)}), f32[32,16,128]{2,1,0:T(8,128)S(1)}, u32[]{:S(2)}, u32[]{:S(2)}) async-start(f32[32,16,128]{2,1,0:T(8,128)} %bitcast.8), calls=%async_computation.1 | async-start | bytes 524288 | tf_op jit(solution)/shard_map/all_to_all | solution.py:141
  99.9 0.1 compare_select_fusion
  100.0 7.8 %collective-permute-done.6 = f32[64,3072]{1,0:T(8,128)S(1)} collective-permute-done((f32[64,3072]{1,0:T(8,128)}, f32[64,3072]{1,0:T(8,128)S(1)}, u32[]{:S(2)}, u32[]{:S(2)}) %collective-permute-start.6) | collective-permute-done | bytes 786464 | tf_op jit(solution)/shard_map/ppermute | solution.py:138
  107.8 0.0 copy-done.1
  107.8 2.6 %select_subtract_fusion = f32[2,64,3072]{2,1,0:T(8,128)} fusion(bf16[2,64,3072]{2,1,0:T(8,128)(2,1)} %param.4, f32[64,3072]{1,0:T(8,128)S(1)} %collective-permute-done.6, f32[64,3072]{1,0:T(8,128)S(1)} %copy-done.1, pred[2]{0:T(512)(128)(4,1)S(1)} %iota_compare_fusion), kind=kLoop, calls=%fused_computation | loop fusion | flops 1179648 | bytes 3932162 | tf_op jit(solution)/shard_map/sub | solution.py:146
  110.4 10.6 %all-to-all-done.1 = f32[32,16,128]{2,1,0:T(8,128)S(1)} async-done(((f32[32,16,128]{2,1,0:T(8,128)}), f32[32,16,128]{2,1,0:T(8,128)S(1)}, u32[]{:S(2)}, u32[]{:S(2)}) %all-to-all-start.1) | async-done | bytes 262176 | tf_op jit(solution)/shard_map/all_to_all | solution.py:141
  121.0 0.3 reshape.68
  121.3 0.2 reduce_sum.9
  121.6 0.6 copy.6
  (10 shorter events, 0.0 us)
Async XLA Ops:
  3.6 9.4 %copy-start.9 = (bf16[2,32,64]{2,1,0:T(8,128)(2,1)S(1)}, bf16[2,32,64]{2,1,0:T(8,128)(2,1)}, u32[]{:S(2)}) copy-start(bf16[2,32,64]{2,1,0:T(8,128)(2,1)} %param.5) | copy-start | bytes 24580
  3.6 60.4 %all-to-all-start = ((bf16[16,64,1536]{2,1,0:T(8,128)(2,1)}), bf16[16,64,1536]{2,1,0:T(8,128)(2,1)S(1)}, u32[]{:S(2)}, u32[]{:S(2)}) async-start(bf16[16,64,1536]{2,1,0:T(8,128)(2,1)} %bitcast.20), calls=%async_computation | async-start | bytes 6291456 | tf_op jit(solution)/shard_map/all_to_all | solution.py:88
  47.2 10.4 %collective-permute-start = (bf16[512,128]{1,0:T(8,128)(2,1)S(1)}, bf16[512,128]{1,0:T(8,128)(2,1)S(1)}, u32[]{:S(2)}, u32[]{:S(2)}) collective-permute-start(bf16[512,128]{1,0:T(8,128)(2,1)S(1)} %all_gather.3.h), channel_id=1, source_target_pairs={{0,16},{16,0},{1,17},{17,1},{2,18},{18,2},{3,19},{19,3},{4,20},{20... | collective-permute-start | bytes 393224 | tf_op jit(solution)/shard_map/ppermute | solution.py:90
  49.8 8.5 %collective-permute-start.1 = (bf16[512,128]{1,0:T(8,128)(2,1)S(1)}, bf16[512,128]{1,0:T(8,128)(2,1)S(1)}, u32[]{:S(2)}, u32[]{:S(2)}) collective-permute-start(bf16[512,128]{1,0:T(8,128)(2,1)S(1)} %all_gather.3.h), channel_id=1, source_target_pairs={{0,8},{8,0},{1,9},{9,1},{2,10},{10,2},{3,11},{11,3},{4,12},{12,4},... | collective-permute-start | bytes 393224 | tf_op jit(solution)/shard_map/ppermute | solution.py:91
  55.3 8.1 %collective-permute-start.2 = (bf16[512,128]{1,0:T(8,128)(2,1)S(1)}, bf16[512,128]{1,0:T(8,128)(2,1)S(1)}, u32[]{:S(2)}, u32[]{:S(2)}) collective-permute-start(bf16[512,128]{1,0:T(8,128)(2,1)S(1)} %all_gather.3.h), channel_id=1, source_target_pairs={{0,24},{8,16},{16,8},{24,0},{1,25},{9,17},{17,9},{25,1},{2,26},{10... | collective-permute-start | bytes 393224 | tf_op jit(solution)/shard_map/ppermute | solution.py:92
  57.6 0.7 copy-start.2
  58.3 0.6 copy-start.4
  63.3 0.6 copy-start.6
  64.0 12.9 %collective-permute-start.5 = (bf16[1024,1536]{1,0:T(8,128)(2,1)S(1)}, bf16[1024,1536]{1,0:T(8,128)(2,1)}, u32[]{:S(2)}, u32[]{:S(2)}) collective-permute-start(bf16[1024,1536]{1,0:T(8,128)(2,1)S(1)} %bitcast.16), channel_id=1, source_target_pairs={{0,1},{1,0},{2,3},{3,2},{4,5},{5,4},{6,7},{7,6},{8,9},{9,8},{10,11... | collective-permute-start | bytes 9437192 | tf_op jit(solution)/shard_map/ppermute | solution.py:110
  67.6 8.2 %copy-start.3 = (bf16[512,128]{1,0:T(8,128)(2,1)S(1)}, bf16[512,128]{1,0:T(8,128)(2,1)}, u32[]{:S(2)}) copy-start(bf16[512,128]{1,0:T(8,128)(2,1)} %copy-done.2) | copy-start | bytes 393220
  67.6 8.2 %copy-start.5 = (bf16[512,128]{1,0:T(8,128)(2,1)S(1)}, bf16[512,128]{1,0:T(8,128)(2,1)}, u32[]{:S(2)}) copy-start(bf16[512,128]{1,0:T(8,128)(2,1)} %copy-done.4) | copy-start | bytes 393220
  67.6 8.2 %copy-start.7 = (bf16[512,128]{1,0:T(8,128)(2,1)S(1)}, bf16[512,128]{1,0:T(8,128)(2,1)}, u32[]{:S(2)}) copy-start(bf16[512,128]{1,0:T(8,128)(2,1)} %copy-done.6) | copy-start | bytes 393220
  67.6 4.7 %collective-permute-start.3 = (f32[16,2,2,16,128]{4,3,2,1,0:T(8,128)S(1)}, f32[16,2,2,16,128]{4,3,2,1,0:T(8,128)S(1)}, u32[]{:S(2)}, u32[]{:S(2)}) collective-permute-start(f32[16,2,2,16,128]{4,3,2,1,0:T(8,128)S(1)} %shard_map.51), channel_id=1, source_target_pairs={{0,1},{1,0},{2,3},{3,2},{4,5},{5,4},{6,7},{7,6},{8,9},{9,8},{10,11... | collective-permute-start | bytes 1572872 | tf_op jit(solution)/shard_map/ppermute | solution.py:111
  73.9 10.2 %collective-permute-start.4 = (f32[16,2,16,128]{3,2,1,0:T(8,128)S(1)}, f32[16,2,16,128]{3,2,1,0:T(8,128)S(1)}, u32[]{:S(2)}, u32[]{:S(2)}) collective-permute-start(f32[16,2,16,128]{3,2,1,0:T(8,128)S(1)} %get-tuple-element.15), channel_id=1, source_target_pairs={{0,16},{16,0},{1,17},{17,1},{2,18},{18,2},{3,19},{19,3},{4,20},{20... | collective-permute-start | bytes 786440 | tf_op jit(solution)/shard_map/ppermute | solution.py:128
  80.7 0.9 copy-start
  84.1 0.7 copy-start.8
  84.1 23.7 %copy-start.1 = (f32[64,3072]{1,0:T(8,128)S(1)}, f32[64,3072]{1,0:T(8,128)}, u32[]{:S(2)}) copy-start(f32[64,3072]{1,0:T(8,128)} %copy-done) | copy-start | bytes 2359300
  84.8 23.0 %collective-permute-start.6 = (f32[64,3072]{1,0:T(8,128)}, f32[64,3072]{1,0:T(8,128)S(1)}, u32[]{:S(2)}, u32[]{:S(2)}) collective-permute-start(f32[64,3072]{1,0:T(8,128)} %get-tuple-element.23), channel_id=1, source_target_pairs={{0,8},{8,0},{1,9},{9,1},{2,10},{10,2},{3,11},{11,3},{4,12},{12,4},... | collective-permute-start | bytes 2359304 | tf_op jit(solution)/shard_map/ppermute | solution.py:138
  88.6 32.4 %all-to-all-start.1 = ((f32[32,16,128]{2,1,0:T(8,128)}), f32[32,16,128]{2,1,0:T(8,128)S(1)}, u32[]{:S(2)}, u32[]{:S(2)}) async-start(f32[32,16,128]{2,1,0:T(8,128)} %bitcast.8), calls=%async_computation.1 | async-start | bytes 524288 | tf_op jit(solution)/shard_map/all_to_all | solution.py:141

commit v4 on v3

--- a/solution.py
+++ b/solution.py
@@ -62,13 +62,32 @@
     factor[...] = jnp.stack(pair, axis=1).reshape(factor.shape)
 
 
-def recon_products(index, mine, core, factor, keep, send):
-    width, half = keep.shape[0], mine.shape[1]
-    for rows, c in ((mine, index[1]), (core, 1 - index[1])):
-        total = lax.dot_general(factor[...], rows[...], (((0,), (0,)), ((), ())), preferred_element_type=jnp.float32)
-        at = pl.ds(pl.multiple_of(c * half, half), half)
-        send[:, at] = total[width:]
-        keep[:, at] = total[:width]
+def recon_here(rows, factor, recon):
+    recon[...] = lax.dot_general(factor[...], rows[...], (((0,), (0,)), ((), ())), preferred_element_type=jnp.float32)
+
+
+def recon_both(index, rows, factor, here, keep, send):
+    width, half = keep.shape[0], rows.shape[1]
+    there = lax.dot_general(factor[...], rows[...], (((0,), (0,)), ((), ())), preferred_element_type=jnp.float32)
+    for at, out in enumerate((keep, send)):
+        run = slice(at * width, (at + 1) * width)
+        out[:, :half] = jnp.where(index[1] == 0, here[run, :], there[run])
+        out[:, half:] = jnp.where(index[1] == 0, there[run], here[run, :])
+
+
+def subtract(yh, target, recon, polar, scratch, sem):
+    scratch[...] = target[yh].astype(jnp.float32) - recon[...]
+    copy = pltpu.make_async_copy(scratch, polar.at[yh], sem)
+    copy.start()
+    copy.wait()
+
+
+def finish_own(index, target, keep, polar, scratch, sem):
+    subtract(index[0], target, keep, polar, scratch, sem)
+
+
+def finish_other(index, target, recon, polar_in, polar, scratch, sem):
+    subtract(1 - index[0], target, recon, polar, scratch, sem)
 
 
 def shards(slab_t, target_t, factor_h):
@@ -107,8 +126,18 @@
         compiler_params=params,
         cost_estimate=cost,
     )(index, mine)
+    core_terms = lax.ppermute(core_terms, "c", SWAP)
+    terms, yl_terms = pl.pallas_call(
+        this_core_gram,
+        out_shape=(row_like, row_like),
+        in_specs=[smem, vmem, vmem],
+        out_specs=(vmem, vmem),
+        compiler_params=params,
+        cost_estimate=cost,
+    )(index, mine, core_terms)
+    terms, yl_terms, mine, h_all = lax.optimization_barrier((terms, yl_terms, mine, h_all))
+    yl_terms = lax.ppermute(yl_terms, "yl", SWAP)
     core = lax.ppermute(mine, "c", SWAP)
-    core_terms = lax.ppermute(core_terms, "c", SWAP)
     factor = pl.pallas_call(
         arrange,
         out_shape=jax.ShapeDtypeStruct((4 * nx * width, 2 * width), slab_t.dtype),
@@ -117,39 +146,50 @@
         compiler_params=params,
         cost_estimate=pl.CostEstimate(flops=0, bytes_accessed=2**20, transcendentals=0),
     )(index, h_all, h_yl, h_yh, h_both)
-    terms, yl_terms = pl.pallas_call(
-        this_core_gram,
-        out_shape=(row_like, row_like),
-        in_specs=[smem, vmem, vmem],
-        out_specs=(vmem, vmem),
-        compiler_params=params,
-        cost_estimate=cost,
-    )(index, mine, core_terms)
-    yl_terms = lax.ppermute(yl_terms, "yl", SWAP)
+    here = pl.pallas_call(
+        recon_here,
+        out_shape=jax.ShapeDtypeStruct((2 * width, half), jnp.float32),
+        in_specs=[vmem] * 2,
+        out_specs=vmem,
+        compiler_params=params,
+        cost_estimate=cost,
+    )(mine, factor)
     keep, send = pl.pallas_call(
-        recon_products,
+        recon_both,
         out_shape=(half_like, half_like),
         in_specs=[smem] + [vmem] * 3,
         out_specs=(vmem,) * 2,
         compiler_params=params,
         cost_estimate=cost,
-    )(index, mine, core, factor)
+    )(index, core, factor, here)
+    recon_other = lax.ppermute(send, "yh", SWAP)
     terms, yl_terms, send = lax.optimization_barrier((terms, yl_terms, send))
-    recon_other = lax.ppermute(send, "yh", SWAP)
     terms = terms + yl_terms
     local = width // 2
     parts = lax.all_to_all(terms.reshape(nrow, width // 4, 2 * width), ("z", "yh"), 0, 0)
     summed = parts.reshape(nz, 2, width // 4, 2, width).sum(0).transpose(2, 1, 0, 3).reshape(local, 2, width)
 
-    slab = jnp.arange(2, dtype=jnp.int32)
-    is_own = (slab == yh)[:, None, None]
-    polar = target_t.astype(jnp.float32) - jnp.where(is_own, keep[None], recon_other[None])
+    def finish(kernel, *args, **kwargs):
+        return pl.pallas_call(
+            kernel,
+            out_shape=jax.ShapeDtypeStruct(target_t.shape, jnp.float32),
+            in_specs=[smem, vmem, vmem] + [anywhere] * (len(args) - 1),
+            out_specs=anywhere,
+            scratch_shapes=[pltpu.VMEM((width, rows), jnp.float32), pltpu.SemaphoreType.DMA],
+            compiler_params=params,
+            cost_estimate=pl.CostEstimate(flops=width * rows, bytes_accessed=10 * width * rows, transcendentals=0),
+            **kwargs,
+        )(index, target_t, *args)
+
+    polar = finish(finish_own, keep)
 
     order_n = rows * nrow
     b_index = lax.axis_index(ROW) * local + jnp.arange(local, dtype=jnp.int32)
     a_index = lax.axis_index(COL) * width + jnp.arange(width, dtype=jnp.int32)
     identity = (b_index[:, None, None] == a_index[None, None, :]).astype(jnp.float32)
     gram = (summed - order_n * identity) * (1.0 / math.sqrt(order_n))
+    gram, recon_other, polar = lax.optimization_barrier((gram, recon_other, polar))
+    polar = finish(finish_other, recon_other, polar, input_output_aliases={3: 0})
     return (gram, polar)
 
 

time: 124 us -> 121 us (0.976)
  local copies, waits for them, and re-layouts: 4.49 us -> 0.98 us
  other arithmetic: 4.72 us -> 1.21 us
  waiting for transfers between devices: 27.5 us -> 30.2 us
  Pallas kernels: 10.9 us -> 12.2 us
    ppermute x1, waiting for transfers between devices: 7.81 us -> 2.48 us  [shards(): recon_other = lax.ppermute(send, 'yh', SWAP)]
    all_to_all x1, waiting for transfers between devices: 10.6 us -> 14.8 us  [shards(): lax.all_to_all(terms.reshape(nrow, width // 4, 2 * width), ('z', 'yh'), 0...]
    unnamed x21 -> x5, local copies, waits for them, and re-layouts: 4.16 us -> 0.65 us
    ppermute x1, starting transfers between devices: 2.07 us -> 5.2 us  [shards(): recon_other = lax.ppermute(send, 'yh', SWAP)]
    all_to_all x1, starting transfers between devices: 11.3 us -> 8.52 us  [shards(): lax.all_to_all(terms.reshape(nrow, width // 4, 2 * width), ('z', 'yh'), 0...]
    sub x1 -> x0, other arithmetic: 2.55 us -> none  [shards(): target_t.astype(jnp.float32)]
    ppermute x1, waiting for transfers between devices: 0.01 us -> 1.55 us  [shards(): core = lax.ppermute(mine, 'c', SWAP)]
    ppermute x1, waiting for transfers between devices: 2.54 us -> 3.82 us  [shards(): yl_terms = lax.ppermute(yl_terms, 'yl', SWAP)]
  transfers between devices with their start and end apart: 9 -> 9, of which waited for: 5 -> 7; matrix products, arithmetic and copies ran while one was open for 4% -> 1% of each run, Pallas kernels for 7% -> 4%
where the time goes in v4:
time: 121 us; the launch traced here: 119 us
  starting transfers between devices  39.4 us (33%)
  blocking collectives  34.1 us (28%)
  waiting for transfers between devices  30.2 us (25%)
  Pallas kernels  12.2 us (10%)
  other arithmetic  1.21 us (1%)
    all_gather x1, blocking collectives, shards(): lax.all_gather(jnp.concatenate([factor_h[0], factor_h[1]], axis=1), 'z',...  34.1 us
    all_to_all x1, waiting for transfers between devices, shards(): lax.all_to_all(terms.reshape(nrow, width // 4, 2 * width), ('z', 'yh'), 0...  14.8 us
    all_to_all x1, starting transfers between devices, shards(): lax.all_to_all(copies.reshape(4 * nx, width, half), COL, 0, 0)  9.43 us
    all_to_all x1, starting transfers between devices, shards(): lax.all_to_all(terms.reshape(nrow, width // 4, 2 * width), ('z', 'yh'), 0...  8.52 us
    ppermute x1, starting transfers between devices, shards(): h_yh = lax.ppermute(h_all, 'yh', SWAP)  5.48 us
    ppermute x1, starting transfers between devices, shards(): recon_other = lax.ppermute(send, 'yh', SWAP)  5.2 us
    ppermute x1, waiting for transfers between devices, shards(): h_both = lax.ppermute(h_all, ('yl', 'yh'), [(i, 3 - i) for i in range(4)])  5.14 us
    ppermute x1, waiting for transfers between devices, shards(): yl_terms = lax.ppermute(yl_terms, 'yl', SWAP)  3.82 us
  transfers between devices with their start and end apart: 9, of which 7 were waited for; matrix products, arithmetic and copies ran while one was open for 1% of the time, Pallas kernels for 4%

profile of v4, /device:TPU:6, one launch (start us, length us, event | category | flops | bytes accessed | tf_op | source)
XLA Modules:
  0.0 119.0 jit_solution(16249246758821555889)
XLA Ops:
  0.6 2.9 %shard_map.50 = bf16[2,4,2,64,1536]{4,3,2,1,0:T(8,128)(2,1)} custom-call(bf16[2,64,3072]{2,1,0:T(8,128)(2,1)} %slab.1), custom_call_target="tpu_custom_call" | custom-call | tf_op jit(solution)/shard_map/pallas_call | solution.py:100
  3.5 0.0 copy-start.1
  3.6 9.4 %all-to-all-start = ((bf16[16,64,1536]{2,1,0:T(8,128)(2,1)}), bf16[16,64,1536]{2,1,0:T(8,128)(2,1)S(1)}, u32[]{:S(2)}, u32[]{:S(2)}) async-start(bf16[16,64,1536]{2,1,0:T(8,128)(2,1)} %bitcast.20), calls=%async_computation | async-start | bytes 6291456 | tf_op jit(solution)/shard_map/all_to_all | solution.py:107
  13.0 0.0 copy-done.1
  13.0 0.1 pad_maximum_fusion
  13.1 34.1 %all_gather.3.h = bf16[512,128]{1,0:T(8,128)(2,1)S(1)} all-gather(bf16[32,128]{1,0:T(8,128)(2,1)S(1)} %pad_maximum_fusion), channel_id=1, replica_groups=mesh['z'=16,'yl'=2,'yh'=2,'x'=4,'c'=2] {'z'}, dimensions={0}, use_global_device_ids=true | all-gather | bytes 139264 | tf_op jit(solution)/shard_map/all_gather | solution.py:108
  47.2 2.6 %collective-permute-start = (bf16[512,128]{1,0:T(8,128)(2,1)S(1)}, bf16[512,128]{1,0:T(8,128)(2,1)S(1)}, u32[]{:S(2)}, u32[]{:S(2)}) collective-permute-start(bf16[512,128]{1,0:T(8,128)(2,1)S(1)} %all_gather.3.h), channel_id=1, source_target_pairs={{0,16},{16,0},{1,17},{17,1},{2,18},{18,2},{3,19},{19,3},{4,20},{20... | collective-permute-start | bytes 393224 | tf_op jit(solution)/shard_map/ppermute | solution.py:109
  49.7 5.5 %collective-permute-start.1 = (bf16[512,128]{1,0:T(8,128)(2,1)S(1)}, bf16[512,128]{1,0:T(8,128)(2,1)S(1)}, u32[]{:S(2)}, u32[]{:S(2)}) collective-permute-start(bf16[512,128]{1,0:T(8,128)(2,1)S(1)} %all_gather.3.h), channel_id=1, source_target_pairs={{0,8},{8,0},{1,9},{9,1},{2,10},{10,2},{3,11},{11,3},{4,12},{12,4},... | collective-permute-start | bytes 393224 | tf_op jit(solution)/shard_map/ppermute | solution.py:110
  55.2 2.4 %collective-permute-start.2 = (bf16[512,128]{1,0:T(8,128)(2,1)S(1)}, bf16[512,128]{1,0:T(8,128)(2,1)}, u32[]{:S(2)}, u32[]{:S(2)}) collective-permute-start(bf16[512,128]{1,0:T(8,128)(2,1)S(1)} %all_gather.3.h), channel_id=1, source_target_pairs={{0,24},{8,16},{16,8},{24,0},{1,25},{9,17},{17,9},{25,1},{2,26},{10... | collective-permute-start | bytes 393224 | tf_op jit(solution)/shard_map/ppermute | solution.py:111
  57.6 0.1 pad_add_fusion.index
  57.7 0.0 collective-permute-done.h_yl
  57.7 0.6 collective-permute-done.1.h_yh
  58.3 5.1 %collective-permute-done.2.h_both = bf16[512,128]{1,0:T(8,128)(2,1)} collective-permute-done((bf16[512,128]{1,0:T(8,128)(2,1)S(1)}, bf16[512,128]{1,0:T(8,128)(2,1)}, u32[]{:S(2)}, u32[]{:S(2)}) %collective-permute-start.2) | collective-permute-done | bytes 131104 | tf_op jit(solution)/shard_map/ppermute | solution.py:111
  63.4 0.0 all-to-all-done
  63.4 1.6 %shard_map.51 = f32[16,2,2,16,128]{4,3,2,1,0:T(8,128)S(1)} custom-call(s32[4]{0:T(128)S(1)} %pad_add_fusion.index, bf16[1024,1536]{1,0:T(8,128)(2,1)S(1)} %bitcast.16), custom_call_target="tpu_custom_call" | custom-call | flops 805306368 | bytes 8388608 | tf_op jit(solution)/shard_map/pallas_call | solution.py:121
  65.0 1.9 %collective-permute-start.3 = (f32[16,2,2,16,128]{4,3,2,1,0:T(8,128)S(1)}, f32[16,2,2,16,128]{4,3,2,1,0:T(8,128)S(1)}, u32[]{:S(2)}, u32[]{:S(2)}) collective-permute-start(f32[16,2,2,16,128]{4,3,2,1,0:T(8,128)S(1)} %shard_map.51), channel_id=1, source_target_pairs={{0,1},{1,0},{2,3},{3,2},{4,5},{5,4},{6,7},{7,6},{8,9},{9,8},{10,11... | collective-permute-start | bytes 1572872 | tf_op jit(solution)/shard_map/ppermute | solution.py:129
  66.9 1.9 %collective-permute-done.3.received = f32[16,2,2,16,128]{4,3,2,1,0:T(8,128)S(1)} collective-permute-done((f32[16,2,2,16,128]{4,3,2,1,0:T(8,128)S(1)}, f32[16,2,2,16,128]{4,3,2,1,0:T(8,128)S(1)}, u32[]{:S(2)}, u32[]{:S(2)}) %collective-permute-start.3) | collective-permute-done | bytes 524320 | tf_op jit(solution)/shard_map/ppermute | solution.py:129
  68.8 1.6 %shard_map.52 = (f32[16,2,16,128]{3,2,1,0:T(8,128)S(1)}, f32[16,2,16,128]{3,2,1,0:T(8,128)S(1)}) custom-call(s32[4]{0:T(128)S(1)} %pad_add_fusion.index, bf16[1024,1536]{1,0:T(8,128)(2,1)S(1)} %bitcast.17, f32[16,2,2,16,128]{4,3,2,1,0:T(8,128)S(1)} %collective-permute-done.3.received), custom_call_target="tpu_custom_call" | custom-call | flops 805306368 | bytes 8388608 | tf_op jit(solution)/shard_map/pallas_call | solution.py:130
  70.4 2.0 %collective-permute-start.5 = (bf16[1024,1536]{1,0:T(8,128)(2,1)S(1)}, bf16[1024,1536]{1,0:T(8,128)(2,1)S(1)}, u32[]{:S(2)}, u32[]{:S(2)}) collective-permute-start(bf16[1024,1536]{1,0:T(8,128)(2,1)S(1)} %bitcast.18), channel_id=1, source_target_pairs={{0,1},{1,0},{2,3},{3,2},{4,5},{5,4},{6,7},{7,6},{8,9},{9,8},{10,11... | collective-permute-start | bytes 9437192 | tf_op jit(solution)/shard_map/ppermute | solution.py:140
  72.5 1.9 %collective-permute-start.4 = (f32[16,2,16,128]{3,2,1,0:T(8,128)S(1)}, f32[16,2,16,128]{3,2,1,0:T(8,128)S(1)}, u32[]{:S(2)}, u32[]{:S(2)}) collective-permute-start(f32[16,2,16,128]{3,2,1,0:T(8,128)S(1)} %get-tuple-element.23), channel_id=1, source_target_pairs={{0,16},{16,0},{1,17},{17,1},{2,18},{18,2},{3,19},{19,3},{4,20},{20... | collective-permute-start | bytes 786440 | tf_op jit(solution)/shard_map/ppermute | solution.py:139
  74.4 1.4 %shard_map.53.factor = bf16[1024,128]{1,0:T(8,128)(2,1)S(1)} custom-call(s32[4]{0:T(128)S(1)} %pad_add_fusion.index, bf16[512,128]{1,0:T(8,128)(2,1)S(1)} %all_gather.3.h, bf16[512,128]{1,0:T(8,128)(2,1)S(1)} %collective-permute-done.h_yl, bf16[512,128]{1,0:T(8,128)(2,1)S(1)} %collective-permute-done.1.h_yh, bf16[512,128]{1,0:T(8,128)(2,1)} %collective-permute-done.2.h_both), custom_call_target="tpu_custom_call" | custom-call | bytes 1048576 | tf_op jit(solution)/shard_map/pallas_call | solution.py:141
  75.8 0.6 shard_map.54.here
  76.4 1.6 %collective-permute-done.5.rows = bf16[1024,1536]{1,0:T(8,128)(2,1)S(1)} collective-permute-done((bf16[1024,1536]{1,0:T(8,128)(2,1)S(1)}, bf16[1024,1536]{1,0:T(8,128)(2,1)S(1)}, u32[]{:S(2)}, u32[]{:S(2)}) %collective-permute-start.5) | collective-permute-done | bytes 3145760 | tf_op jit(solution)/shard_map/ppermute | solution.py:140
  78.0 0.0 copy-start
  78.0 1.1 shard_map.55
  79.1 3.8 %collective-permute-done.4 = f32[16,2,16,128]{3,2,1,0:T(8,128)S(1)} collective-permute-done((f32[16,2,16,128]{3,2,1,0:T(8,128)S(1)}, f32[16,2,16,128]{3,2,1,0:T(8,128)S(1)}, u32[]{:S(2)}, u32[]{:S(2)}) %collective-permute-start.4) | collective-permute-done | bytes 262176 | tf_op jit(solution)/shard_map/ppermute | solution.py:139
  82.9 0.7 add.32
  83.7 8.5 %all-to-all-start.1 = ((f32[32,16,128]{2,1,0:T(8,128)}), f32[32,16,128]{2,1,0:T(8,128)S(1)}, u32[]{:S(2)}, u32[]{:S(2)}) async-start(f32[32,16,128]{2,1,0:T(8,128)} %bitcast.8), calls=%async_computation.1 | async-start | bytes 524288 | tf_op jit(solution)/shard_map/all_to_all | solution.py:169
  92.2 5.2 %collective-permute-start.6 = (f32[64,3072]{1,0:T(8,128)S(1)}, f32[64,3072]{1,0:T(8,128)S(1)}, u32[]{:S(2)}, u32[]{:S(2)}) collective-permute-start(f32[64,3072]{1,0:T(8,128)S(1)} %get-tuple-element.29), channel_id=1, source_target_pairs={{0,8},{8,0},{1,9},{9,1},{2,10},{10,2},{3,11},{11,3},{4,12},{12,4},... | collective-permute-start | bytes 2359304 | tf_op jit(solution)/shard_map/ppermute | solution.py:165
  97.4 0.1 compare_select_fusion
  97.5 0.0 copy-done
  97.5 1.5 %shard_map.56.polar_in = f32[2,64,3072]{2,1,0:T(8,128)} custom-call(s32[4]{0:T(128)S(1)} %pad_add_fusion.index, bf16[2,64,3072]{2,1,0:T(8,128)(2,1)S(1)} %copy-done, f32[64,3072]{1,0:T(8,128)S(1)} %get-tuple-element.32.keep), custom_call_target="tpu_custom_call" | custom-call | flops 196608 | bytes 1966080 | tf_op jit(solution)/shard_map/pallas_call | solution.py:173
  99.0 14.8 %all-to-all-done.1 = f32[32,16,128]{2,1,0:T(8,128)S(1)} async-done(((f32[32,16,128]{2,1,0:T(8,128)}), f32[32,16,128]{2,1,0:T(8,128)S(1)}, u32[]{:S(2)}, u32[]{:S(2)}) %all-to-all-start.1) | async-done | bytes 262176 | tf_op jit(solution)/shard_map/all_to_all | solution.py:169
  113.8 0.3 reshape.62
  114.1 0.2 reduce_sum.9
  114.4 2.5 %collective-permute-done.6.recon = f32[64,3072]{1,0:T(8,128)S(1)} collective-permute-done((f32[64,3072]{1,0:T(8,128)S(1)}, f32[64,3072]{1,0:T(8,128)S(1)}, u32[]{:S(2)}, u32[]{:S(2)}) %collective-permute-start.6) | collective-permute-done | bytes 786464 | tf_op jit(solution)/shard_map/ppermute | solution.py:165
  116.9 0.6 copy.7
  117.5 1.5 %shard_map.57 = f32[2,64,3072]{2,1,0:T(8,128)} custom-call(s32[4]{0:T(128)S(1)} %pad_add_fusion.index, bf16[2,64,3072]{2,1,0:T(8,128)(2,1)S(1)} %copy-done, f32[64,3072]{1,0:T(8,128)S(1)} %collective-permute-done.6.recon, f32[2,64,3072]{2,1,0:T(8,128)} %shard_map.56.polar_in), custom_call_target="tpu_custom_call", output_to_operand_aliasing={{}: (3, {})} | custom-call | flops 196608 | bytes 1966080 | tf_op jit(solution)/shard_map/pallas_call | solution.py:173
  (5 shorter events, 0.0 us)
Async XLA Ops:
  3.5 9.4 %copy-start.1 = (bf16[2,32,64]{2,1,0:T(8,128)(2,1)S(1)}, bf16[2,32,64]{2,1,0:T(8,128)(2,1)}, u32[]{:S(2)}) copy-start(bf16[2,32,64]{2,1,0:T(8,128)(2,1)} %param.5) | copy-start | bytes 24580
  3.6 59.9 %all-to-all-start = ((bf16[16,64,1536]{2,1,0:T(8,128)(2,1)}), bf16[16,64,1536]{2,1,0:T(8,128)(2,1)S(1)}, u32[]{:S(2)}, u32[]{:S(2)}) async-start(bf16[16,64,1536]{2,1,0:T(8,128)(2,1)} %bitcast.20), calls=%async_computation | async-start | bytes 6291456 | tf_op jit(solution)/shard_map/all_to_all | solution.py:107
  47.2 10.5 %collective-permute-start = (bf16[512,128]{1,0:T(8,128)(2,1)S(1)}, bf16[512,128]{1,0:T(8,128)(2,1)S(1)}, u32[]{:S(2)}, u32[]{:S(2)}) collective-permute-start(bf16[512,128]{1,0:T(8,128)(2,1)S(1)} %all_gather.3.h), channel_id=1, source_target_pairs={{0,16},{16,0},{1,17},{17,1},{2,18},{18,2},{3,19},{19,3},{4,20},{20... | collective-permute-start | bytes 393224 | tf_op jit(solution)/shard_map/ppermute | solution.py:109
  49.7 8.5 %collective-permute-start.1 = (bf16[512,128]{1,0:T(8,128)(2,1)S(1)}, bf16[512,128]{1,0:T(8,128)(2,1)S(1)}, u32[]{:S(2)}, u32[]{:S(2)}) collective-permute-start(bf16[512,128]{1,0:T(8,128)(2,1)S(1)} %all_gather.3.h), channel_id=1, source_target_pairs={{0,8},{8,0},{1,9},{9,1},{2,10},{10,2},{3,11},{11,3},{4,12},{12,4},... | collective-permute-start | bytes 393224 | tf_op jit(solution)/shard_map/ppermute | solution.py:110
  55.2 8.2 %collective-permute-start.2 = (bf16[512,128]{1,0:T(8,128)(2,1)S(1)}, bf16[512,128]{1,0:T(8,128)(2,1)}, u32[]{:S(2)}, u32[]{:S(2)}) collective-permute-start(bf16[512,128]{1,0:T(8,128)(2,1)S(1)} %all_gather.3.h), channel_id=1, source_target_pairs={{0,24},{8,16},{16,8},{24,0},{1,25},{9,17},{17,9},{25,1},{2,26},{10... | collective-permute-start | bytes 393224 | tf_op jit(solution)/shard_map/ppermute | solution.py:111
  65.0 3.8 %collective-permute-start.3 = (f32[16,2,2,16,128]{4,3,2,1,0:T(8,128)S(1)}, f32[16,2,2,16,128]{4,3,2,1,0:T(8,128)S(1)}, u32[]{:S(2)}, u32[]{:S(2)}) collective-permute-start(f32[16,2,2,16,128]{4,3,2,1,0:T(8,128)S(1)} %shard_map.51), channel_id=1, source_target_pairs={{0,1},{1,0},{2,3},{3,2},{4,5},{5,4},{6,7},{7,6},{8,9},{9,8},{10,11... | collective-permute-start | bytes 1572872 | tf_op jit(solution)/shard_map/ppermute | solution.py:129
  70.4 7.6 %collective-permute-start.5 = (bf16[1024,1536]{1,0:T(8,128)(2,1)S(1)}, bf16[1024,1536]{1,0:T(8,128)(2,1)S(1)}, u32[]{:S(2)}, u32[]{:S(2)}) collective-permute-start(bf16[1024,1536]{1,0:T(8,128)(2,1)S(1)} %bitcast.18), channel_id=1, source_target_pairs={{0,1},{1,0},{2,3},{3,2},{4,5},{5,4},{6,7},{7,6},{8,9},{9,8},{10,11... | collective-permute-start | bytes 9437192 | tf_op jit(solution)/shard_map/ppermute | solution.py:140
  72.5 10.5 %collective-permute-start.4 = (f32[16,2,16,128]{3,2,1,0:T(8,128)S(1)}, f32[16,2,16,128]{3,2,1,0:T(8,128)S(1)}, u32[]{:S(2)}, u32[]{:S(2)}) collective-permute-start(f32[16,2,16,128]{3,2,1,0:T(8,128)S(1)} %get-tuple-element.23), channel_id=1, source_target_pairs={{0,16},{16,0},{1,17},{17,1},{2,18},{18,2},{3,19},{19,3},{4,20},{20... | collective-permute-start | bytes 786440 | tf_op jit(solution)/shard_map/ppermute | solution.py:139
  78.0 19.6 %copy-start = (bf16[2,64,3072]{2,1,0:T(8,128)(2,1)S(1)}, bf16[2,64,3072]{2,1,0:T(8,128)(2,1)}, u32[]{:S(2)}) copy-start(bf16[2,64,3072]{2,1,0:T(8,128)(2,1)} %target.3) | copy-start | bytes 2359300
  83.7 30.1 %all-to-all-start.1 = ((f32[32,16,128]{2,1,0:T(8,128)}), f32[32,16,128]{2,1,0:T(8,128)S(1)}, u32[]{:S(2)}, u32[]{:S(2)}) async-start(f32[32,16,128]{2,1,0:T(8,128)} %bitcast.8), calls=%async_computation.1 | async-start | bytes 524288 | tf_op jit(solution)/shard_map/all_to_all | solution.py:169
  92.2 24.7 %collective-permute-start.6 = (f32[64,3072]{1,0:T(8,128)S(1)}, f32[64,3072]{1,0:T(8,128)S(1)}, u32[]{:S(2)}, u32[]{:S(2)}) collective-permute-start(f32[64,3072]{1,0:T(8,128)S(1)} %get-tuple-element.29), channel_id=1, source_target_pairs={{0,8},{8,0},{1,9},{9,1},{2,10},{10,2},{3,11},{11,3},{4,12},{12,4},... | collective-permute-start | bytes 2359304 | tf_op jit(solution)/shard_map/ppermute | solution.py:165

commit v5 on v4

--- a/solution.py
+++ b/solution.py
@@ -106,10 +106,10 @@
     )(slab_t)
     mine = lax.all_to_all(copies.reshape(4 * nx, width, half), COL, 0, 0).reshape(4 * nx * width, half)
     h_all = lax.all_gather(jnp.concatenate([factor_h[0], factor_h[1]], axis=1), "z", axis=0, tiled=True)
+    h_both = lax.ppermute(h_all, ("yl", "yh"), [(i, 3 - i) for i in range(4)])
+    h_yh = lax.ppermute(h_all, "yh", SWAP)
     h_yl = lax.ppermute(h_all, "yl", SWAP)
-    h_yh = lax.ppermute(h_all, "yh", SWAP)
-    h_both = lax.ppermute(h_all, ("yl", "yh"), [(i, 3 - i) for i in range(4)])
-    mine, h_yl, h_yh, h_both = lax.optimization_barrier((mine, h_yl, h_yh, h_both))
+    mine, h_both, h_yh, h_yl = lax.optimization_barrier((mine, h_both, h_yh, h_yl))
 
     index = jnp.stack([yh, c, x, yl]).astype(jnp.int32)
     params = pltpu.CompilerParams(vmem_limit_bytes=14 * 2**20)
@@ -166,8 +166,7 @@
     terms, yl_terms, send = lax.optimization_barrier((terms, yl_terms, send))
     terms = terms + yl_terms
     local = width // 2
-    parts = lax.all_to_all(terms.reshape(nrow, width // 4, 2 * width), ("z", "yh"), 0, 0)
-    summed = parts.reshape(nz, 2, width // 4, 2, width).sum(0).transpose(2, 1, 0, 3).reshape(local, 2, width)
+    parts = lax.all_to_all(terms, "z", 0, 0)
 
     def finish(kernel, *args, **kwargs):
         return pl.pallas_call(
@@ -182,14 +181,21 @@
         )(index, target_t, *args)
 
     polar = finish(finish_own, keep)
+    parts, polar = lax.optimization_barrier((parts, polar))
+    parts = parts.sum(0)
+    own_part = lax.dynamic_index_in_dim(parts, yh, 0, keepdims=False)
+    other_part = lax.ppermute(lax.dynamic_index_in_dim(parts, 1 - yh, 0, keepdims=False), "yh", SWAP)
+    own_part, recon_other, polar = lax.optimization_barrier((own_part, recon_other, polar))
+    polar = finish(finish_other, recon_other, polar, input_output_aliases={3: 0})
+    is_own = (jnp.arange(2, dtype=jnp.int32) == yh)[:, None, None]
+    parts = jnp.where(is_own, own_part[None], other_part[None])
+    summed = parts.reshape(2, width // 4, 2, width).transpose(2, 1, 0, 3).reshape(local, 2, width)
 
     order_n = rows * nrow
     b_index = lax.axis_index(ROW) * local + jnp.arange(local, dtype=jnp.int32)
     a_index = lax.axis_index(COL) * width + jnp.arange(width, dtype=jnp.int32)
     identity = (b_index[:, None, None] == a_index[None, None, :]).astype(jnp.float32)
     gram = (summed - order_n * identity) * (1.0 / math.sqrt(order_n))
-    gram, recon_other, polar = lax.optimization_barrier((gram, recon_other, polar))
-    polar = finish(finish_other, recon_other, polar, input_output_aliases={3: 0})
     return (gram, polar)
 
 

time: 121 us -> 118 us (0.975)
  waiting for transfers between devices: 30.2 us -> 25.4 us
  starting transfers between devices: 39.4 us -> 42.1 us
    ppermute x1, waiting for transfers between devices: 5.14 us -> 0.01 us  [shards(): h_both = lax.ppermute(h_all, ('yl', 'yh'), [(i, 3 - i) for i in range(4)])]
    ppermute x1, starting transfers between devices: 5.48 us -> 2.1 us  [shards(): h_yh = lax.ppermute(h_all, 'yh', SWAP)]
    ppermute x0 -> x1, starting transfers between devices: none -> 3.35 us  [shards(): lax.ppermute(lax.dynamic_index_in_dim(parts, 1 - yh, 0, keepdims=False),...]
    ppermute x1, waiting for transfers between devices: 0.59 us -> 3.14 us  [shards(): h_yh = lax.ppermute(h_all, 'yh', SWAP)]
    ppermute x1, starting transfers between devices: 2.35 us -> 4.69 us  [shards(): h_both = lax.ppermute(h_all, ('yl', 'yh'), [(i, 3 - i) for i in range(4)])]
    ppermute x1, waiting for transfers between devices: 2.48 us -> 0.54 us  [shards(): recon_other = lax.ppermute(send, 'yh', SWAP)]
    ppermute x1, starting transfers between devices: 5.2 us -> 3.33 us  [shards(): recon_other = lax.ppermute(send, 'yh', SWAP)]
    ppermute x0 -> x1, waiting for transfers between devices: none -> 1.55 us  [shards(): lax.ppermute(lax.dynamic_index_in_dim(parts, 1 - yh, 0, keepdims=False),...]
  transfers between devices with their start and end apart: 9 -> 10, of which waited for: 7 -> 8; matrix products, arithmetic and copies ran while one was open for 1% -> 0% of each run, Pallas kernels for 4% -> 5%
where the time goes in v5:
time: 118 us; the launch traced here: 117 us
  starting transfers between devices  42.1 us (36%)
  blocking collectives  34.1 us (29%)
  waiting for transfers between devices  25.4 us (22%)
  Pallas kernels  12.2 us (10%)
  other arithmetic  1.71 us (1%)
    all_gather x1, blocking collectives, shards(): lax.all_gather(jnp.concatenate([factor_h[0], factor_h[1]], axis=1), 'z',...  34.1 us
    all_to_all x1, waiting for transfers between devices, shards(): parts = lax.all_to_all(terms, 'z', 0, 0)  13.3 us
    all_to_all x1, starting transfers between devices, shards(): lax.all_to_all(copies.reshape(4 * nx, width, half), COL, 0, 0)  9.43 us
    all_to_all x1, starting transfers between devices, shards(): parts = lax.all_to_all(terms, 'z', 0, 0)  9.22 us
    ppermute x1, starting transfers between devices, shards(): h_both = lax.ppermute(h_all, ('yl', 'yh'), [(i, 3 - i) for i in range(4)])  4.69 us
    ppermute x1, waiting for transfers between devices, shards(): yl_terms = lax.ppermute(yl_terms, 'yl', SWAP)  3.82 us
    ppermute x1, starting transfers between devices, shards(): lax.ppermute(lax.dynamic_index_in_dim(parts, 1 - yh, 0, keepdims=False),...  3.35 us
    ppermute x1, starting transfers between devices, shards(): recon_other = lax.ppermute(send, 'yh', SWAP)  3.33 us
  transfers between devices with their start and end apart: 10, of which 8 were waited for; matrix products, arithmetic and copies ran while one was open for 0% of the time, Pallas kernels for 5%

profile of v5, /device:TPU:6, one launch (start us, length us, event | category | flops | bytes accessed | tf_op | source)
XLA Modules:
  0.0 116.6 jit_solution(9033959800313962231)
XLA Ops:
  0.6 2.9 %shard_map.50 = bf16[2,4,2,64,1536]{4,3,2,1,0:T(8,128)(2,1)} custom-call(bf16[2,64,3072]{2,1,0:T(8,128)(2,1)} %slab.1), custom_call_target="tpu_custom_call" | custom-call | tf_op jit(solution)/shard_map/pallas_call | solution.py:100
  3.6 0.0 copy-start.1
  3.6 9.4 %all-to-all-start = ((bf16[16,64,1536]{2,1,0:T(8,128)(2,1)}), bf16[16,64,1536]{2,1,0:T(8,128)(2,1)S(1)}, u32[]{:S(2)}, u32[]{:S(2)}) async-start(bf16[16,64,1536]{2,1,0:T(8,128)(2,1)} %bitcast.22), calls=%async_computation | async-start | bytes 6291456 | tf_op jit(solution)/shard_map/all_to_all | solution.py:107
  13.0 0.0 copy-done.1
  13.0 0.1 pad_maximum_fusion
  13.1 34.1 %all_gather.3.h = bf16[512,128]{1,0:T(8,128)(2,1)S(1)} all-gather(bf16[32,128]{1,0:T(8,128)(2,1)S(1)} %pad_maximum_fusion), channel_id=1, replica_groups=mesh['z'=16,'yl'=2,'yh'=2,'x'=4,'c'=2] {'z'}, dimensions={0}, use_global_device_ids=true | all-gather | bytes 139264 | tf_op jit(solution)/shard_map/all_gather | solution.py:108
  47.2 4.7 %collective-permute-start = (bf16[512,128]{1,0:T(8,128)(2,1)S(1)}, bf16[512,128]{1,0:T(8,128)(2,1)S(1)}, u32[]{:S(2)}, u32[]{:S(2)}) collective-permute-start(bf16[512,128]{1,0:T(8,128)(2,1)S(1)} %all_gather.3.h), channel_id=1, source_target_pairs={{0,24},{8,16},{16,8},{24,0},{1,25},{9,17},{17,9},{25,1},{2,26},{10... | collective-permute-start | bytes 393224 | tf_op jit(solution)/shard_map/ppermute | solution.py:109
  51.9 2.1 %collective-permute-start.1 = (bf16[512,128]{1,0:T(8,128)(2,1)S(1)}, bf16[512,128]{1,0:T(8,128)(2,1)S(1)}, u32[]{:S(2)}, u32[]{:S(2)}) collective-permute-start(bf16[512,128]{1,0:T(8,128)(2,1)S(1)} %all_gather.3.h), channel_id=1, source_target_pairs={{0,8},{8,0},{1,9},{9,1},{2,10},{10,2},{3,11},{11,3},{4,12},{12,4},... | collective-permute-start | bytes 393224 | tf_op jit(solution)/shard_map/ppermute | solution.py:110
  54.0 3.0 %collective-permute-start.2 = (bf16[512,128]{1,0:T(8,128)(2,1)S(1)}, bf16[512,128]{1,0:T(8,128)(2,1)}, u32[]{:S(2)}, u32[]{:S(2)}) collective-permute-start(bf16[512,128]{1,0:T(8,128)(2,1)S(1)} %all_gather.3.h), channel_id=1, source_target_pairs={{0,16},{16,0},{1,17},{17,1},{2,18},{18,2},{3,19},{19,3},{4,20},{20... | collective-permute-start | bytes 393224 | tf_op jit(solution)/shard_map/ppermute | solution.py:111
  57.0 0.1 pad_add_fusion.index
  57.1 0.0 collective-permute-done.h_both
  57.1 3.1 %collective-permute-done.1.h_yh = bf16[512,128]{1,0:T(8,128)(2,1)S(1)} collective-permute-done((bf16[512,128]{1,0:T(8,128)(2,1)S(1)}, bf16[512,128]{1,0:T(8,128)(2,1)S(1)}, u32[]{:S(2)}, u32[]{:S(2)}) %collective-permute-start.1) | collective-permute-done | bytes 131104 | tf_op jit(solution)/shard_map/ppermute | solution.py:110
  60.2 0.7 collective-permute-done.2.h_yl
  60.9 0.0 all-to-all-done
  60.9 1.6 %shard_map.51 = f32[16,2,2,16,128]{4,3,2,1,0:T(8,128)S(1)} custom-call(s32[4]{0:T(128)S(1)} %pad_add_fusion.index, bf16[1024,1536]{1,0:T(8,128)(2,1)S(1)} %bitcast.18), custom_call_target="tpu_custom_call" | custom-call | flops 805306368 | bytes 8388608 | tf_op jit(solution)/shard_map/pallas_call | solution.py:121
  62.5 1.9 %collective-permute-start.3 = (f32[16,2,2,16,128]{4,3,2,1,0:T(8,128)S(1)}, f32[16,2,2,16,128]{4,3,2,1,0:T(8,128)S(1)}, u32[]{:S(2)}, u32[]{:S(2)}) collective-permute-start(f32[16,2,2,16,128]{4,3,2,1,0:T(8,128)S(1)} %shard_map.51), channel_id=1, source_target_pairs={{0,1},{1,0},{2,3},{3,2},{4,5},{5,4},{6,7},{7,6},{8,9},{9,8},{10,11... | collective-permute-start | bytes 1572872 | tf_op jit(solution)/shard_map/ppermute | solution.py:129
  64.5 1.9 %collective-permute-done.3.received = f32[16,2,2,16,128]{4,3,2,1,0:T(8,128)S(1)} collective-permute-done((f32[16,2,2,16,128]{4,3,2,1,0:T(8,128)S(1)}, f32[16,2,2,16,128]{4,3,2,1,0:T(8,128)S(1)}, u32[]{:S(2)}, u32[]{:S(2)}) %collective-permute-start.3) | collective-permute-done | bytes 524320 | tf_op jit(solution)/shard_map/ppermute | solution.py:129
  66.3 1.6 %shard_map.52 = (f32[16,2,16,128]{3,2,1,0:T(8,128)S(1)}, f32[16,2,16,128]{3,2,1,0:T(8,128)S(1)}) custom-call(s32[4]{0:T(128)S(1)} %pad_add_fusion.index, bf16[1024,1536]{1,0:T(8,128)(2,1)S(1)} %bitcast.19, f32[16,2,2,16,128]{4,3,2,1,0:T(8,128)S(1)} %collective-permute-done.3.received), custom_call_target="tpu_custom_call" | custom-call | flops 805306368 | bytes 8388608 | tf_op jit(solution)/shard_map/pallas_call | solution.py:130
  67.9 2.0 %collective-permute-start.5 = (bf16[1024,1536]{1,0:T(8,128)(2,1)S(1)}, bf16[1024,1536]{1,0:T(8,128)(2,1)S(1)}, u32[]{:S(2)}, u32[]{:S(2)}) collective-permute-start(bf16[1024,1536]{1,0:T(8,128)(2,1)S(1)} %bitcast.20), channel_id=1, source_target_pairs={{0,1},{1,0},{2,3},{3,2},{4,5},{5,4},{6,7},{7,6},{8,9},{9,8},{10,11... | collective-permute-start | bytes 9437192 | tf_op jit(solution)/shard_map/ppermute | solution.py:140
  70.0 3.0 %collective-permute-start.4 = (f32[16,2,16,128]{3,2,1,0:T(8,128)S(1)}, f32[16,2,16,128]{3,2,1,0:T(8,128)S(1)}, u32[]{:S(2)}, u32[]{:S(2)}) collective-permute-start(f32[16,2,16,128]{3,2,1,0:T(8,128)S(1)} %get-tuple-element.25), channel_id=1, source_target_pairs={{0,16},{16,0},{1,17},{17,1},{2,18},{18,2},{3,19},{19,3},{4,20},{20... | collective-permute-start | bytes 786440 | tf_op jit(solution)/shard_map/ppermute | solution.py:139
  73.0 1.4 %shard_map.53.factor = bf16[1024,128]{1,0:T(8,128)(2,1)S(1)} custom-call(s32[4]{0:T(128)S(1)} %pad_add_fusion.index, bf16[512,128]{1,0:T(8,128)(2,1)S(1)} %all_gather.3.h, bf16[512,128]{1,0:T(8,128)(2,1)} %collective-permute-done.2.h_yl, bf16[512,128]{1,0:T(8,128)(2,1)S(1)} %collective-permute-done.1.h_yh, bf16[512,128]{1,0:T(8,128)(2,1)S(1)} %collective-permute-done.h_both), custom_call_target="tpu_custom_call" | custom-call | bytes 1048576 | tf_op jit(solution)/shard_map/pallas_call | solution.py:141
  74.4 0.6 shard_map.54.here
  75.0 0.4 collective-permute-done.5.rows
  75.5 0.0 copy-start
  75.5 1.1 shard_map.55
  76.6 3.8 %collective-permute-done.4 = f32[16,2,16,128]{3,2,1,0:T(8,128)S(1)} collective-permute-done((f32[16,2,16,128]{3,2,1,0:T(8,128)S(1)}, f32[16,2,16,128]{3,2,1,0:T(8,128)S(1)}, u32[]{:S(2)}, u32[]{:S(2)}) %collective-permute-start.4) | collective-permute-done | bytes 262176 | tf_op jit(solution)/shard_map/ppermute | solution.py:139
  80.5 0.7 add.40
  81.2 9.2 %all-to-all-start.1 = ((f32[16,2,16,128]{3,2,1,0:T(8,128)}), f32[16,2,16,128]{3,2,1,0:T(8,128)S(1)}, u32[]{:S(2)}, u32[]{:S(2)}) async-start(f32[16,2,16,128]{3,2,1,0:T(8,128)} %add.40), calls=%async_computation.1 | async-start | bytes 524288 | tf_op jit(solution)/shard_map/all_to_all | solution.py:169
  90.4 3.3 %collective-permute-start.6 = (f32[64,3072]{1,0:T(8,128)S(1)}, f32[64,3072]{1,0:T(8,128)S(1)}, u32[]{:S(2)}, u32[]{:S(2)}) collective-permute-start(f32[64,3072]{1,0:T(8,128)S(1)} %get-tuple-element.31), channel_id=1, source_target_pairs={{0,8},{8,0},{1,9},{9,1},{2,10},{10,2},{3,11},{11,3},{4,12},{12,4},... | collective-permute-start | bytes 2359304 | tf_op jit(solution)/shard_map/ppermute | solution.py:165
  93.8 0.1 compare_select_fusion
  93.9 0.0 copy-done
  93.9 1.5 %shard_map.56.polar_in = f32[2,64,3072]{2,1,0:T(8,128)} custom-call(s32[4]{0:T(128)S(1)} %pad_add_fusion.index, bf16[2,64,3072]{2,1,0:T(8,128)(2,1)S(1)} %copy-done, f32[64,3072]{1,0:T(8,128)S(1)} %get-tuple-element.34.keep), custom_call_target="tpu_custom_call" | custom-call | flops 196608 | bytes 1966080 | tf_op jit(solution)/shard_map/pallas_call | solution.py:172
  95.4 13.3 %all-to-all-done.1 = f32[16,2,16,128]{3,2,1,0:T(8,128)S(1)} async-done(((f32[16,2,16,128]{3,2,1,0:T(8,128)}), f32[16,2,16,128]{3,2,1,0:T(8,128)S(1)}, u32[]{:S(2)}, u32[]{:S(2)}) %all-to-all-start.1) | async-done | bytes 262176 | tf_op jit(solution)/shard_map/all_to_all | solution.py:169
  108.7 3.4 %collective-permute-start.7 = (f32[16,128]{1,0:T(8,128)S(1)}, f32[16,128]{1,0:T(8,128)S(1)}, u32[]{:S(2)}, u32[]{:S(2)}) collective-permute-start(f32[16,128]{1,0:T(8,128)S(1)} %get-tuple-element.41), channel_id=1, source_target_pairs={{0,8},{8,0},{1,9},{9,1},{2,10},{10,2},{3,11},{11,3},{4,12},{12,4},... | collective-permute-start | bytes 24584 | tf_op jit(solution)/shard_map/ppermute | solution.py:187
  112.1 0.5 collective-permute-done.6.recon
  112.6 1.5 %shard_map.57 = f32[2,64,3072]{2,1,0:T(8,128)} custom-call(s32[4]{0:T(128)S(1)} %pad_add_fusion.index, bf16[2,64,3072]{2,1,0:T(8,128)(2,1)S(1)} %copy-done, f32[64,3072]{1,0:T(8,128)S(1)} %collective-permute-done.6.recon, f32[2,64,3072]{2,1,0:T(8,128)} %shard_map.56.polar_in), custom_call_target="tpu_custom_call", output_to_operand_aliasing={{}: (3, {})} | custom-call | flops 196608 | bytes 1966080 | tf_op jit(solution)/shard_map/pallas_call | solution.py:172
  114.1 0.1 broadcast_in_dim.42
  114.2 1.5 %collective-permute-done.7 = f32[16,128]{1,0:T(8,128)S(1)} collective-permute-done((f32[16,128]{1,0:T(8,128)S(1)}, f32[16,128]{1,0:T(8,128)S(1)}, u32[]{:S(2)}, u32[]{:S(2)}) %collective-permute-start.7) | collective-permute-done | bytes 8224 | tf_op jit(solution)/shard_map/ppermute | solution.py:187
  115.8 0.1 broadcast_in_dim.46
  115.9 0.7 subtract_multiply_fusion
  (8 shorter events, 0.1 us)
Async XLA Ops:
  3.6 9.4 %copy-start.1 = (bf16[2,32,64]{2,1,0:T(8,128)(2,1)S(1)}, bf16[2,32,64]{2,1,0:T(8,128)(2,1)}, u32[]{:S(2)}) copy-start(bf16[2,32,64]{2,1,0:T(8,128)(2,1)} %param.5) | copy-start | bytes 24580
  3.6 57.4 %all-to-all-start = ((bf16[16,64,1536]{2,1,0:T(8,128)(2,1)}), bf16[16,64,1536]{2,1,0:T(8,128)(2,1)S(1)}, u32[]{:S(2)}, u32[]{:S(2)}) async-start(bf16[16,64,1536]{2,1,0:T(8,128)(2,1)} %bitcast.22), calls=%async_computation | async-start | bytes 6291456 | tf_op jit(solution)/shard_map/all_to_all | solution.py:107
  47.2 9.9 %collective-permute-start = (bf16[512,128]{1,0:T(8,128)(2,1)S(1)}, bf16[512,128]{1,0:T(8,128)(2,1)S(1)}, u32[]{:S(2)}, u32[]{:S(2)}) collective-permute-start(bf16[512,128]{1,0:T(8,128)(2,1)S(1)} %all_gather.3.h), channel_id=1, source_target_pairs={{0,24},{8,16},{16,8},{24,0},{1,25},{9,17},{17,9},{25,1},{2,26},{10... | collective-permute-start | bytes 393224 | tf_op jit(solution)/shard_map/ppermute | solution.py:109
  51.9 8.4 %collective-permute-start.1 = (bf16[512,128]{1,0:T(8,128)(2,1)S(1)}, bf16[512,128]{1,0:T(8,128)(2,1)S(1)}, u32[]{:S(2)}, u32[]{:S(2)}) collective-permute-start(bf16[512,128]{1,0:T(8,128)(2,1)S(1)} %all_gather.3.h), channel_id=1, source_target_pairs={{0,8},{8,0},{1,9},{9,1},{2,10},{10,2},{3,11},{11,3},{4,12},{12,4},... | collective-permute-start | bytes 393224 | tf_op jit(solution)/shard_map/ppermute | solution.py:110
  54.0 7.0 %collective-permute-start.2 = (bf16[512,128]{1,0:T(8,128)(2,1)S(1)}, bf16[512,128]{1,0:T(8,128)(2,1)}, u32[]{:S(2)}, u32[]{:S(2)}) collective-permute-start(bf16[512,128]{1,0:T(8,128)(2,1)S(1)} %all_gather.3.h), channel_id=1, source_target_pairs={{0,16},{16,0},{1,17},{17,1},{2,18},{18,2},{3,19},{19,3},{4,20},{20... | collective-permute-start | bytes 393224 | tf_op jit(solution)/shard_map/ppermute | solution.py:111
  62.5 3.8 %collective-permute-start.3 = (f32[16,2,2,16,128]{4,3,2,1,0:T(8,128)S(1)}, f32[16,2,2,16,128]{4,3,2,1,0:T(8,128)S(1)}, u32[]{:S(2)}, u32[]{:S(2)}) collective-permute-start(f32[16,2,2,16,128]{4,3,2,1,0:T(8,128)S(1)} %shard_map.51), channel_id=1, source_target_pairs={{0,1},{1,0},{2,3},{3,2},{4,5},{5,4},{6,7},{7,6},{8,9},{9,8},{10,11... | collective-permute-start | bytes 1572872 | tf_op jit(solution)/shard_map/ppermute | solution.py:129
  67.9 7.6 %collective-permute-start.5 = (bf16[1024,1536]{1,0:T(8,128)(2,1)S(1)}, bf16[1024,1536]{1,0:T(8,128)(2,1)S(1)}, u32[]{:S(2)}, u32[]{:S(2)}) collective-permute-start(bf16[1024,1536]{1,0:T(8,128)(2,1)S(1)} %bitcast.20), channel_id=1, source_target_pairs={{0,1},{1,0},{2,3},{3,2},{4,5},{5,4},{6,7},{7,6},{8,9},{9,8},{10,11... | collective-permute-start | bytes 9437192 | tf_op jit(solution)/shard_map/ppermute | solution.py:140
  70.0 10.5 %collective-permute-start.4 = (f32[16,2,16,128]{3,2,1,0:T(8,128)S(1)}, f32[16,2,16,128]{3,2,1,0:T(8,128)S(1)}, u32[]{:S(2)}, u32[]{:S(2)}) collective-permute-start(f32[16,2,16,128]{3,2,1,0:T(8,128)S(1)} %get-tuple-element.25), channel_id=1, source_target_pairs={{0,16},{16,0},{1,17},{17,1},{2,18},{18,2},{3,19},{19,3},{4,20},{20... | collective-permute-start | bytes 786440 | tf_op jit(solution)/shard_map/ppermute | solution.py:139
  75.5 18.4 %copy-start = (bf16[2,64,3072]{2,1,0:T(8,128)(2,1)S(1)}, bf16[2,64,3072]{2,1,0:T(8,128)(2,1)}, u32[]{:S(2)}) copy-start(bf16[2,64,3072]{2,1,0:T(8,128)(2,1)} %target.3) | copy-start | bytes 2359300
  81.2 27.5 %all-to-all-start.1 = ((f32[16,2,16,128]{3,2,1,0:T(8,128)}), f32[16,2,16,128]{3,2,1,0:T(8,128)S(1)}, u32[]{:S(2)}, u32[]{:S(2)}) async-start(f32[16,2,16,128]{3,2,1,0:T(8,128)} %add.40), calls=%async_computation.1 | async-start | bytes 524288 | tf_op jit(solution)/shard_map/all_to_all | solution.py:169
  90.4 22.2 %collective-permute-start.6 = (f32[64,3072]{1,0:T(8,128)S(1)}, f32[64,3072]{1,0:T(8,128)S(1)}, u32[]{:S(2)}, u32[]{:S(2)}) collective-permute-start(f32[64,3072]{1,0:T(8,128)S(1)} %get-tuple-element.31), channel_id=1, source_target_pairs={{0,8},{8,0},{1,9},{9,1},{2,10},{10,2},{3,11},{11,3},{4,12},{12,4},... | collective-permute-start | bytes 2359304 | tf_op jit(solution)/shard_map/ppermute | solution.py:165
  108.7 7.0 %collective-permute-start.7 = (f32[16,128]{1,0:T(8,128)S(1)}, f32[16,128]{1,0:T(8,128)S(1)}, u32[]{:S(2)}, u32[]{:S(2)}) collective-permute-start(f32[16,128]{1,0:T(8,128)S(1)} %get-tuple-element.41), channel_id=1, source_target_pairs={{0,8},{8,0},{1,9},{9,1},{2,10},{10,2},{3,11},{11,3},{4,12},{12,4},... | collective-permute-start | bytes 24584 | tf_op jit(solution)/shard_map/ppermute | solution.py:187

commit v6 on v5

--- a/solution.py
+++ b/solution.py
@@ -15,13 +15,18 @@
 SWAP = [(0, 1), (1, 0)]
 
 
-def spread(slab, copies, sems):
+def spread(slab, copies, pieces, load_sems, sems):
     half = copies.shape[4]
-    started = []
-    for yh, x, c in itertools.product(*map(range, copies.shape[:3])):
+    loads, started = [], []
+    for yh, c in itertools.product(range(2), range(2)):
         source = slab.at[yh, :, pl.ds(c * half, half)]
-        started.append(pltpu.make_async_copy(source, copies.at[yh, x, c], sems.at[len(started)]))
-        started[-1].start()
+        loads.append((yh, c, pltpu.make_async_copy(source, pieces.at[yh, c], load_sems.at[len(loads)])))
+        loads[-1][2].start()
+    for yh, c, load in loads:
+        load.wait()
+        for x in range(copies.shape[1]):
+            started.append(pltpu.make_async_copy(pieces.at[yh, c], copies.at[yh, x, c], sems.at[len(started)]))
+            started[-1].start()
     for copy in started:
         copy.wait()
 
@@ -100,9 +105,13 @@
     copies = pl.pallas_call(
         spread,
         out_shape=jax.ShapeDtypeStruct((2, nx, 2, width, half), slab_t.dtype),
-        in_specs=[vmem],
+        in_specs=[anywhere],
         out_specs=anywhere,
-        scratch_shapes=[pltpu.SemaphoreType.DMA((4 * nx,))],
+        scratch_shapes=[
+            pltpu.VMEM((2, 2, width, half), slab_t.dtype),
+            pltpu.SemaphoreType.DMA((4,)),
+            pltpu.SemaphoreType.DMA((4 * nx,)),
+        ],
     )(slab_t)
     mine = lax.all_to_all(copies.reshape(4 * nx, width, half), COL, 0, 0).reshape(4 * nx * width, half)
     h_all = lax.all_gather(jnp.concatenate([factor_h[0], factor_h[1]], axis=1), "z", axis=0, tiled=True)

time: 118 us -> 118 us (level)
  no operation moved by 1% of the time
where the time goes in v6:
time: 118 us; the launch traced here: 116 us
  starting transfers between devices  42.1 us (36%)
  blocking collectives  34.1 us (29%)
  waiting for transfers between devices  25.4 us (22%)
  Pallas kernels  12 us (10%)
  other arithmetic  1.71 us (1%)
    all_gather x1, blocking collectives, shards(): lax.all_gather(jnp.concatenate([factor_h[0], factor_h[1]], axis=1), 'z',...  34.1 us
    all_to_all x1, waiting for transfers between devices, shards(): parts = lax.all_to_all(terms, 'z', 0, 0)  13.3 us
    all_to_all x1, starting transfers between devices, shards(): lax.all_to_all(copies.reshape(4 * nx, width, half), COL, 0, 0)  9.43 us
    all_to_all x1, starting transfers between devices, shards(): parts = lax.all_to_all(terms, 'z', 0, 0)  9.25 us
    ppermute x1, starting transfers between devices, shards(): h_both = lax.ppermute(h_all, ('yl', 'yh'), [(i, 3 - i) for i in range(4)])  4.69 us
    ppermute x1, waiting for transfers between devices, shards(): yl_terms = lax.ppermute(yl_terms, 'yl', SWAP)  3.82 us
    ppermute x1, starting transfers between devices, shards(): recon_other = lax.ppermute(send, 'yh', SWAP)  3.33 us
    ppermute x1, starting transfers between devices, shards(): lax.ppermute(lax.dynamic_index_in_dim(parts, 1 - yh, 0, keepdims=False),...  3.33 us
  transfers between devices with their start and end apart: 10, of which 8 were waited for; matrix products, arithmetic and copies ran while one was open for 0% of the time, Pallas kernels for 5%

profile of v6, /device:TPU:6, one launch (start us, length us, event | category | flops | bytes accessed | tf_op | source)
XLA Modules:
  0.0 116.4 jit_solution(4290967931144030495)
XLA Ops:
  0.6 2.7 %shard_map.50 = bf16[2,4,2,64,1536]{4,3,2,1,0:T(8,128)(2,1)} custom-call(bf16[2,64,3072]{2,1,0:T(8,128)(2,1)} %slab.1), custom_call_target="tpu_custom_call" | custom-call | tf_op jit(solution)/shard_map/pallas_call | solution.py:105
  3.4 0.0 copy-start.1
  3.4 9.4 %all-to-all-start = ((bf16[16,64,1536]{2,1,0:T(8,128)(2,1)}), bf16[16,64,1536]{2,1,0:T(8,128)(2,1)S(1)}, u32[]{:S(2)}, u32[]{:S(2)}) async-start(bf16[16,64,1536]{2,1,0:T(8,128)(2,1)} %bitcast.22), calls=%async_computation | async-start | bytes 6291456 | tf_op jit(solution)/shard_map/all_to_all | solution.py:116
  12.8 0.0 copy-done.1
  12.8 0.1 pad_maximum_fusion
  12.9 34.1 %all_gather.3.h = bf16[512,128]{1,0:T(8,128)(2,1)S(1)} all-gather(bf16[32,128]{1,0:T(8,128)(2,1)S(1)} %pad_maximum_fusion), channel_id=1, replica_groups=mesh['z'=16,'yl'=2,'yh'=2,'x'=4,'c'=2] {'z'}, dimensions={0}, use_global_device_ids=true | all-gather | bytes 139264 | tf_op jit(solution)/shard_map/all_gather | solution.py:117
  47.0 4.7 %collective-permute-start = (bf16[512,128]{1,0:T(8,128)(2,1)S(1)}, bf16[512,128]{1,0:T(8,128)(2,1)S(1)}, u32[]{:S(2)}, u32[]{:S(2)}) collective-permute-start(bf16[512,128]{1,0:T(8,128)(2,1)S(1)} %all_gather.3.h), channel_id=1, source_target_pairs={{0,24},{8,16},{16,8},{24,0},{1,25},{9,17},{17,9},{25,1},{2,26},{10... | collective-permute-start | bytes 393224 | tf_op jit(solution)/shard_map/ppermute | solution.py:118
  51.7 2.1 %collective-permute-start.1 = (bf16[512,128]{1,0:T(8,128)(2,1)S(1)}, bf16[512,128]{1,0:T(8,128)(2,1)S(1)}, u32[]{:S(2)}, u32[]{:S(2)}) collective-permute-start(bf16[512,128]{1,0:T(8,128)(2,1)S(1)} %all_gather.3.h), channel_id=1, source_target_pairs={{0,8},{8,0},{1,9},{9,1},{2,10},{10,2},{3,11},{11,3},{4,12},{12,4},... | collective-permute-start | bytes 393224 | tf_op jit(solution)/shard_map/ppermute | solution.py:119
  53.8 3.0 %collective-permute-start.2 = (bf16[512,128]{1,0:T(8,128)(2,1)S(1)}, bf16[512,128]{1,0:T(8,128)(2,1)}, u32[]{:S(2)}, u32[]{:S(2)}) collective-permute-start(bf16[512,128]{1,0:T(8,128)(2,1)S(1)} %all_gather.3.h), channel_id=1, source_target_pairs={{0,16},{16,0},{1,17},{17,1},{2,18},{18,2},{3,19},{19,3},{4,20},{20... | collective-permute-start | bytes 393224 | tf_op jit(solution)/shard_map/ppermute | solution.py:120
  56.8 0.1 pad_add_fusion.index
  56.9 0.0 collective-permute-done.h_both
  56.9 3.1 %collective-permute-done.1.h_yh = bf16[512,128]{1,0:T(8,128)(2,1)S(1)} collective-permute-done((bf16[512,128]{1,0:T(8,128)(2,1)S(1)}, bf16[512,128]{1,0:T(8,128)(2,1)S(1)}, u32[]{:S(2)}, u32[]{:S(2)}) %collective-permute-start.1) | collective-permute-done | bytes 131104 | tf_op jit(solution)/shard_map/ppermute | solution.py:119
  60.0 0.7 collective-permute-done.2.h_yl
  60.8 0.0 all-to-all-done
  60.8 1.6 %shard_map.51 = f32[16,2,2,16,128]{4,3,2,1,0:T(8,128)S(1)} custom-call(s32[4]{0:T(128)S(1)} %pad_add_fusion.index, bf16[1024,1536]{1,0:T(8,128)(2,1)S(1)} %bitcast.18), custom_call_target="tpu_custom_call" | custom-call | flops 805306368 | bytes 8388608 | tf_op jit(solution)/shard_map/pallas_call | solution.py:130
  62.3 1.9 %collective-permute-start.3 = (f32[16,2,2,16,128]{4,3,2,1,0:T(8,128)S(1)}, f32[16,2,2,16,128]{4,3,2,1,0:T(8,128)S(1)}, u32[]{:S(2)}, u32[]{:S(2)}) collective-permute-start(f32[16,2,2,16,128]{4,3,2,1,0:T(8,128)S(1)} %shard_map.51), channel_id=1, source_target_pairs={{0,1},{1,0},{2,3},{3,2},{4,5},{5,4},{6,7},{7,6},{8,9},{9,8},{10,11... | collective-permute-start | bytes 1572872 | tf_op jit(solution)/shard_map/ppermute | solution.py:138
  64.3 1.9 %collective-permute-done.3.received = f32[16,2,2,16,128]{4,3,2,1,0:T(8,128)S(1)} collective-permute-done((f32[16,2,2,16,128]{4,3,2,1,0:T(8,128)S(1)}, f32[16,2,2,16,128]{4,3,2,1,0:T(8,128)S(1)}, u32[]{:S(2)}, u32[]{:S(2)}) %collective-permute-start.3) | collective-permute-done | bytes 524320 | tf_op jit(solution)/shard_map/ppermute | solution.py:138
  66.1 1.6 %shard_map.52 = (f32[16,2,16,128]{3,2,1,0:T(8,128)S(1)}, f32[16,2,16,128]{3,2,1,0:T(8,128)S(1)}) custom-call(s32[4]{0:T(128)S(1)} %pad_add_fusion.index, bf16[1024,1536]{1,0:T(8,128)(2,1)S(1)} %bitcast.19, f32[16,2,2,16,128]{4,3,2,1,0:T(8,128)S(1)} %collective-permute-done.3.received), custom_call_target="tpu_custom_call" | custom-call | flops 805306368 | bytes 8388608 | tf_op jit(solution)/shard_map/pallas_call | solution.py:139
  67.7 2.1 %collective-permute-start.5 = (bf16[1024,1536]{1,0:T(8,128)(2,1)S(1)}, bf16[1024,1536]{1,0:T(8,128)(2,1)S(1)}, u32[]{:S(2)}, u32[]{:S(2)}) collective-permute-start(bf16[1024,1536]{1,0:T(8,128)(2,1)S(1)} %bitcast.20), channel_id=1, source_target_pairs={{0,1},{1,0},{2,3},{3,2},{4,5},{5,4},{6,7},{7,6},{8,9},{9,8},{10,11... | collective-permute-start | bytes 9437192 | tf_op jit(solution)/shard_map/ppermute | solution.py:149
  69.8 3.0 %collective-permute-start.4 = (f32[16,2,16,128]{3,2,1,0:T(8,128)S(1)}, f32[16,2,16,128]{3,2,1,0:T(8,128)S(1)}, u32[]{:S(2)}, u32[]{:S(2)}) collective-permute-start(f32[16,2,16,128]{3,2,1,0:T(8,128)S(1)} %get-tuple-element.25), channel_id=1, source_target_pairs={{0,16},{16,0},{1,17},{17,1},{2,18},{18,2},{3,19},{19,3},{4,20},{20... | collective-permute-start | bytes 786440 | tf_op jit(solution)/shard_map/ppermute | solution.py:148
  72.8 1.4 %shard_map.53.factor = bf16[1024,128]{1,0:T(8,128)(2,1)S(1)} custom-call(s32[4]{0:T(128)S(1)} %pad_add_fusion.index, bf16[512,128]{1,0:T(8,128)(2,1)S(1)} %all_gather.3.h, bf16[512,128]{1,0:T(8,128)(2,1)} %collective-permute-done.2.h_yl, bf16[512,128]{1,0:T(8,128)(2,1)S(1)} %collective-permute-done.1.h_yh, bf16[512,128]{1,0:T(8,128)(2,1)S(1)} %collective-permute-done.h_both), custom_call_target="tpu_custom_call" | custom-call | bytes 1048576 | tf_op jit(solution)/shard_map/pallas_call | solution.py:150
  74.2 0.6 shard_map.54.here
  74.9 0.4 collective-permute-done.5.rows
  75.3 0.0 copy-start
  75.3 1.1 shard_map.55
  76.4 3.8 %collective-permute-done.4 = f32[16,2,16,128]{3,2,1,0:T(8,128)S(1)} collective-permute-done((f32[16,2,16,128]{3,2,1,0:T(8,128)S(1)}, f32[16,2,16,128]{3,2,1,0:T(8,128)S(1)}, u32[]{:S(2)}, u32[]{:S(2)}) %collective-permute-start.4) | collective-permute-done | bytes 262176 | tf_op jit(solution)/shard_map/ppermute | solution.py:148
  80.3 0.7 add.40
  81.0 9.2 %all-to-all-start.1 = ((f32[16,2,16,128]{3,2,1,0:T(8,128)}), f32[16,2,16,128]{3,2,1,0:T(8,128)S(1)}, u32[]{:S(2)}, u32[]{:S(2)}) async-start(f32[16,2,16,128]{3,2,1,0:T(8,128)} %add.40), calls=%async_computation.1 | async-start | bytes 524288 | tf_op jit(solution)/shard_map/all_to_all | solution.py:178
  90.3 3.3 %collective-permute-start.6 = (f32[64,3072]{1,0:T(8,128)S(1)}, f32[64,3072]{1,0:T(8,128)S(1)}, u32[]{:S(2)}, u32[]{:S(2)}) collective-permute-start(f32[64,3072]{1,0:T(8,128)S(1)} %get-tuple-element.31), channel_id=1, source_target_pairs={{0,8},{8,0},{1,9},{9,1},{2,10},{10,2},{3,11},{11,3},{4,12},{12,4},... | collective-permute-start | bytes 2359304 | tf_op jit(solution)/shard_map/ppermute | solution.py:174
  93.6 0.1 compare_select_fusion
  93.7 0.0 copy-done
  93.7 1.5 %shard_map.56.polar_in = f32[2,64,3072]{2,1,0:T(8,128)} custom-call(s32[4]{0:T(128)S(1)} %pad_add_fusion.index, bf16[2,64,3072]{2,1,0:T(8,128)(2,1)S(1)} %copy-done, f32[64,3072]{1,0:T(8,128)S(1)} %get-tuple-element.34.keep), custom_call_target="tpu_custom_call" | custom-call | flops 196608 | bytes 1966080 | tf_op jit(solution)/shard_map/pallas_call | solution.py:181
  95.2 13.3 %all-to-all-done.1 = f32[16,2,16,128]{3,2,1,0:T(8,128)S(1)} async-done(((f32[16,2,16,128]{3,2,1,0:T(8,128)}), f32[16,2,16,128]{3,2,1,0:T(8,128)S(1)}, u32[]{:S(2)}, u32[]{:S(2)}) %all-to-all-start.1) | async-done | bytes 262176 | tf_op jit(solution)/shard_map/all_to_all | solution.py:178
  108.6 3.3 %collective-permute-start.7 = (f32[16,128]{1,0:T(8,128)S(1)}, f32[16,128]{1,0:T(8,128)S(1)}, u32[]{:S(2)}, u32[]{:S(2)}) collective-permute-start(f32[16,128]{1,0:T(8,128)S(1)} %get-tuple-element.41), channel_id=1, source_target_pairs={{0,8},{8,0},{1,9},{9,1},{2,10},{10,2},{3,11},{11,3},{4,12},{12,4},... | collective-permute-start | bytes 24584 | tf_op jit(solution)/shard_map/ppermute | solution.py:196
  111.9 0.6 collective-permute-done.6.recon
  112.5 1.5 %shard_map.57 = f32[2,64,3072]{2,1,0:T(8,128)} custom-call(s32[4]{0:T(128)S(1)} %pad_add_fusion.index, bf16[2,64,3072]{2,1,0:T(8,128)(2,1)S(1)} %copy-done, f32[64,3072]{1,0:T(8,128)S(1)} %collective-permute-done.6.recon, f32[2,64,3072]{2,1,0:T(8,128)} %shard_map.56.polar_in), custom_call_target="tpu_custom_call", output_to_operand_aliasing={{}: (3, {})} | custom-call | flops 196608 | bytes 1966080 | tf_op jit(solution)/shard_map/pallas_call | solution.py:181
  114.0 0.1 broadcast_in_dim.42
  114.1 1.6 %collective-permute-done.7 = f32[16,128]{1,0:T(8,128)S(1)} collective-permute-done((f32[16,128]{1,0:T(8,128)S(1)}, f32[16,128]{1,0:T(8,128)S(1)}, u32[]{:S(2)}, u32[]{:S(2)}) %collective-permute-start.7) | collective-permute-done | bytes 8224 | tf_op jit(solution)/shard_map/ppermute | solution.py:196
  115.6 0.1 broadcast_in_dim.46
  115.7 0.7 subtract_multiply_fusion
  (8 shorter events, 0.1 us)
Async XLA Ops:
  3.4 9.4 %copy-start.1 = (bf16[2,32,64]{2,1,0:T(8,128)(2,1)S(1)}, bf16[2,32,64]{2,1,0:T(8,128)(2,1)}, u32[]{:S(2)}) copy-start(bf16[2,32,64]{2,1,0:T(8,128)(2,1)} %param.5) | copy-start | bytes 24580
  3.4 57.4 %all-to-all-start = ((bf16[16,64,1536]{2,1,0:T(8,128)(2,1)}), bf16[16,64,1536]{2,1,0:T(8,128)(2,1)S(1)}, u32[]{:S(2)}, u32[]{:S(2)}) async-start(bf16[16,64,1536]{2,1,0:T(8,128)(2,1)} %bitcast.22), calls=%async_computation | async-start | bytes 6291456 | tf_op jit(solution)/shard_map/all_to_all | solution.py:116
  47.0 9.9 %collective-permute-start = (bf16[512,128]{1,0:T(8,128)(2,1)S(1)}, bf16[512,128]{1,0:T(8,128)(2,1)S(1)}, u32[]{:S(2)}, u32[]{:S(2)}) collective-permute-start(bf16[512,128]{1,0:T(8,128)(2,1)S(1)} %all_gather.3.h), channel_id=1, source_target_pairs={{0,24},{8,16},{16,8},{24,0},{1,25},{9,17},{17,9},{25,1},{2,26},{10... | collective-permute-start | bytes 393224 | tf_op jit(solution)/shard_map/ppermute | solution.py:118
  51.7 8.4 %collective-permute-start.1 = (bf16[512,128]{1,0:T(8,128)(2,1)S(1)}, bf16[512,128]{1,0:T(8,128)(2,1)S(1)}, u32[]{:S(2)}, u32[]{:S(2)}) collective-permute-start(bf16[512,128]{1,0:T(8,128)(2,1)S(1)} %all_gather.3.h), channel_id=1, source_target_pairs={{0,8},{8,0},{1,9},{9,1},{2,10},{10,2},{3,11},{11,3},{4,12},{12,4},... | collective-permute-start | bytes 393224 | tf_op jit(solution)/shard_map/ppermute | solution.py:119
  53.8 7.0 %collective-permute-start.2 = (bf16[512,128]{1,0:T(8,128)(2,1)S(1)}, bf16[512,128]{1,0:T(8,128)(2,1)}, u32[]{:S(2)}, u32[]{:S(2)}) collective-permute-start(bf16[512,128]{1,0:T(8,128)(2,1)S(1)} %all_gather.3.h), channel_id=1, source_target_pairs={{0,16},{16,0},{1,17},{17,1},{2,18},{18,2},{3,19},{19,3},{4,20},{20... | collective-permute-start | bytes 393224 | tf_op jit(solution)/shard_map/ppermute | solution.py:120
  62.3 3.8 %collective-permute-start.3 = (f32[16,2,2,16,128]{4,3,2,1,0:T(8,128)S(1)}, f32[16,2,2,16,128]{4,3,2,1,0:T(8,128)S(1)}, u32[]{:S(2)}, u32[]{:S(2)}) collective-permute-start(f32[16,2,2,16,128]{4,3,2,1,0:T(8,128)S(1)} %shard_map.51), channel_id=1, source_target_pairs={{0,1},{1,0},{2,3},{3,2},{4,5},{5,4},{6,7},{7,6},{8,9},{9,8},{10,11... | collective-permute-start | bytes 1572872 | tf_op jit(solution)/shard_map/ppermute | solution.py:138
  67.7 7.6 %collective-permute-start.5 = (bf16[1024,1536]{1,0:T(8,128)(2,1)S(1)}, bf16[1024,1536]{1,0:T(8,128)(2,1)S(1)}, u32[]{:S(2)}, u32[]{:S(2)}) collective-permute-start(bf16[1024,1536]{1,0:T(8,128)(2,1)S(1)} %bitcast.20), channel_id=1, source_target_pairs={{0,1},{1,0},{2,3},{3,2},{4,5},{5,4},{6,7},{7,6},{8,9},{9,8},{10,11... | collective-permute-start | bytes 9437192 | tf_op jit(solution)/shard_map/ppermute | solution.py:149
  69.8 10.5 %collective-permute-start.4 = (f32[16,2,16,128]{3,2,1,0:T(8,128)S(1)}, f32[16,2,16,128]{3,2,1,0:T(8,128)S(1)}, u32[]{:S(2)}, u32[]{:S(2)}) collective-permute-start(f32[16,2,16,128]{3,2,1,0:T(8,128)S(1)} %get-tuple-element.25), channel_id=1, source_target_pairs={{0,16},{16,0},{1,17},{17,1},{2,18},{18,2},{3,19},{19,3},{4,20},{20... | collective-permute-start | bytes 786440 | tf_op jit(solution)/shard_map/ppermute | solution.py:148
  75.3 18.4 %copy-start = (bf16[2,64,3072]{2,1,0:T(8,128)(2,1)S(1)}, bf16[2,64,3072]{2,1,0:T(8,128)(2,1)}, u32[]{:S(2)}) copy-start(bf16[2,64,3072]{2,1,0:T(8,128)(2,1)} %target.3) | copy-start | bytes 2359300
  81.0 27.5 %all-to-all-start.1 = ((f32[16,2,16,128]{3,2,1,0:T(8,128)}), f32[16,2,16,128]{3,2,1,0:T(8,128)S(1)}, u32[]{:S(2)}, u32[]{:S(2)}) async-start(f32[16,2,16,128]{3,2,1,0:T(8,128)} %add.40), calls=%async_computation.1 | async-start | bytes 524288 | tf_op jit(solution)/shard_map/all_to_all | solution.py:178
  90.3 22.2 %collective-permute-start.6 = (f32[64,3072]{1,0:T(8,128)S(1)}, f32[64,3072]{1,0:T(8,128)S(1)}, u32[]{:S(2)}, u32[]{:S(2)}) collective-permute-start(f32[64,3072]{1,0:T(8,128)S(1)} %get-tuple-element.31), channel_id=1, source_target_pairs={{0,8},{8,0},{1,9},{9,1},{2,10},{10,2},{3,11},{11,3},{4,12},{12,4},... | collective-permute-start | bytes 2359304 | tf_op jit(solution)/shard_map/ppermute | solution.py:174
  108.6 7.0 %collective-permute-start.7 = (f32[16,128]{1,0:T(8,128)S(1)}, f32[16,128]{1,0:T(8,128)S(1)}, u32[]{:S(2)}, u32[]{:S(2)}) collective-permute-start(f32[16,128]{1,0:T(8,128)S(1)} %get-tuple-element.41), channel_id=1, source_target_pairs={{0,8},{8,0},{1,9},{9,1},{2,10},{10,2},{3,11},{11,3},{4,12},{12,4},... | collective-permute-start | bytes 24584 | tf_op jit(solution)/shard_map/ppermute | solution.py:196

commit v7 on v6

--- a/solution.py
+++ b/solution.py
@@ -81,10 +81,15 @@
 
 
 def subtract(yh, target, recon, polar, scratch, sem):
-    scratch[...] = target[yh].astype(jnp.float32) - recon[...]
-    copy = pltpu.make_async_copy(scratch, polar.at[yh], sem)
-    copy.start()
-    copy.wait()
+    size = scratch.shape[0] // 4
+    copies = []
+    for part in range(4):
+        run = pl.ds(part * size, size)
+        scratch[run, :] = target[yh, run, :].astype(jnp.float32) - recon[run, :]
+        copies.append(pltpu.make_async_copy(scratch.at[run, :], polar.at[yh, run, :], sem.at[part]))
+        copies[-1].start()
+    for copy in copies:
+        copy.wait()
 
 
 def finish_own(index, target, keep, polar, scratch, sem):
@@ -183,7 +188,7 @@
             out_shape=jax.ShapeDtypeStruct(target_t.shape, jnp.float32),
             in_specs=[smem, vmem, vmem] + [anywhere] * (len(args) - 1),
             out_specs=anywhere,
-            scratch_shapes=[pltpu.VMEM((width, rows), jnp.float32), pltpu.SemaphoreType.DMA],
+            scratch_shapes=[pltpu.VMEM((width, rows), jnp.float32), pltpu.SemaphoreType.DMA((4,))],
             compiler_params=params,
             cost_estimate=pl.CostEstimate(flops=width * rows, bytes_accessed=10 * width * rows, transcendentals=0),
             **kwargs,

time: 118 us -> 118 us (level)
  no operation moved by 1% of the time
where the time goes in v7:
time: 118 us; the launch traced here: 116 us
  starting transfers between devices  42.1 us (36%)
  blocking collectives  34.1 us (29%)
  waiting for transfers between devices  25.5 us (22%)
  Pallas kernels  12 us (10%)
  other arithmetic  1.71 us (1%)
    all_gather x1, blocking collectives, shards(): lax.all_gather(jnp.concatenate([factor_h[0], factor_h[1]], axis=1), 'z',...  34.1 us
    all_to_all x1, waiting for transfers between devices, shards(): parts = lax.all_to_all(terms, 'z', 0, 0)  13.3 us
    all_to_all x1, starting transfers between devices, shards(): lax.all_to_all(copies.reshape(4 * nx, width, half), COL, 0, 0)  9.43 us
    all_to_all x1, starting transfers between devices, shards(): parts = lax.all_to_all(terms, 'z', 0, 0)  9.25 us
    ppermute x1, starting transfers between devices, shards(): h_both = lax.ppermute(h_all, ('yl', 'yh'), [(i, 3 - i) for i in range(4)])  4.69 us
    ppermute x1, waiting for transfers between devices, shards(): yl_terms = lax.ppermute(yl_terms, 'yl', SWAP)  3.82 us
    ppermute x1, starting transfers between devices, shards(): recon_other = lax.ppermute(send, 'yh', SWAP)  3.33 us
    ppermute x1, starting transfers between devices, shards(): lax.ppermute(lax.dynamic_index_in_dim(parts, 1 - yh, 0, keepdims=False),...  3.33 us
  transfers between devices with their start and end apart: 10, of which 8 were waited for; matrix products, arithmetic and copies ran while one was open for 0% of the time, Pallas kernels for 5%

profile of v7, /device:TPU:6, one launch (start us, length us, event | category | flops | bytes accessed | tf_op | source)
XLA Modules:
  0.0 116.4 jit_solution(14350751366298397959)
XLA Ops:
  0.6 2.7 %shard_map.50 = bf16[2,4,2,64,1536]{4,3,2,1,0:T(8,128)(2,1)} custom-call(bf16[2,64,3072]{2,1,0:T(8,128)(2,1)} %slab.1), custom_call_target="tpu_custom_call" | custom-call | tf_op jit(solution)/shard_map/pallas_call | solution.py:110
  3.4 0.0 copy-start.1
  3.4 9.4 %all-to-all-start = ((bf16[16,64,1536]{2,1,0:T(8,128)(2,1)}), bf16[16,64,1536]{2,1,0:T(8,128)(2,1)S(1)}, u32[]{:S(2)}, u32[]{:S(2)}) async-start(bf16[16,64,1536]{2,1,0:T(8,128)(2,1)} %bitcast.22), calls=%async_computation | async-start | bytes 6291456 | tf_op jit(solution)/shard_map/all_to_all | solution.py:121
  12.8 0.0 copy-done.1
  12.8 0.1 pad_maximum_fusion
  12.9 34.1 %all_gather.3.h = bf16[512,128]{1,0:T(8,128)(2,1)S(1)} all-gather(bf16[32,128]{1,0:T(8,128)(2,1)S(1)} %pad_maximum_fusion), channel_id=1, replica_groups=mesh['z'=16,'yl'=2,'yh'=2,'x'=4,'c'=2] {'z'}, dimensions={0}, use_global_device_ids=true | all-gather | bytes 139264 | tf_op jit(solution)/shard_map/all_gather | solution.py:122
  47.0 4.7 %collective-permute-start = (bf16[512,128]{1,0:T(8,128)(2,1)S(1)}, bf16[512,128]{1,0:T(8,128)(2,1)S(1)}, u32[]{:S(2)}, u32[]{:S(2)}) collective-permute-start(bf16[512,128]{1,0:T(8,128)(2,1)S(1)} %all_gather.3.h), channel_id=1, source_target_pairs={{0,24},{8,16},{16,8},{24,0},{1,25},{9,17},{17,9},{25,1},{2,26},{10... | collective-permute-start | bytes 393224 | tf_op jit(solution)/shard_map/ppermute | solution.py:123
  51.7 2.1 %collective-permute-start.1 = (bf16[512,128]{1,0:T(8,128)(2,1)S(1)}, bf16[512,128]{1,0:T(8,128)(2,1)S(1)}, u32[]{:S(2)}, u32[]{:S(2)}) collective-permute-start(bf16[512,128]{1,0:T(8,128)(2,1)S(1)} %all_gather.3.h), channel_id=1, source_target_pairs={{0,8},{8,0},{1,9},{9,1},{2,10},{10,2},{3,11},{11,3},{4,12},{12,4},... | collective-permute-start | bytes 393224 | tf_op jit(solution)/shard_map/ppermute | solution.py:124
  53.8 3.0 %collective-permute-start.2 = (bf16[512,128]{1,0:T(8,128)(2,1)S(1)}, bf16[512,128]{1,0:T(8,128)(2,1)}, u32[]{:S(2)}, u32[]{:S(2)}) collective-permute-start(bf16[512,128]{1,0:T(8,128)(2,1)S(1)} %all_gather.3.h), channel_id=1, source_target_pairs={{0,16},{16,0},{1,17},{17,1},{2,18},{18,2},{3,19},{19,3},{4,20},{20... | collective-permute-start | bytes 393224 | tf_op jit(solution)/shard_map/ppermute | solution.py:125
  56.8 0.1 pad_add_fusion.index
  56.9 0.0 collective-permute-done.h_both
  56.9 3.1 %collective-permute-done.1.h_yh = bf16[512,128]{1,0:T(8,128)(2,1)S(1)} collective-permute-done((bf16[512,128]{1,0:T(8,128)(2,1)S(1)}, bf16[512,128]{1,0:T(8,128)(2,1)S(1)}, u32[]{:S(2)}, u32[]{:S(2)}) %collective-permute-start.1) | collective-permute-done | bytes 131104 | tf_op jit(solution)/shard_map/ppermute | solution.py:124
  60.0 0.7 collective-permute-done.2.h_yl
  60.8 0.0 all-to-all-done
  60.8 1.6 %shard_map.51 = f32[16,2,2,16,128]{4,3,2,1,0:T(8,128)S(1)} custom-call(s32[4]{0:T(128)S(1)} %pad_add_fusion.index, bf16[1024,1536]{1,0:T(8,128)(2,1)S(1)} %bitcast.18), custom_call_target="tpu_custom_call" | custom-call | flops 805306368 | bytes 8388608 | tf_op jit(solution)/shard_map/pallas_call | solution.py:135
  62.3 1.9 %collective-permute-start.3 = (f32[16,2,2,16,128]{4,3,2,1,0:T(8,128)S(1)}, f32[16,2,2,16,128]{4,3,2,1,0:T(8,128)S(1)}, u32[]{:S(2)}, u32[]{:S(2)}) collective-permute-start(f32[16,2,2,16,128]{4,3,2,1,0:T(8,128)S(1)} %shard_map.51), channel_id=1, source_target_pairs={{0,1},{1,0},{2,3},{3,2},{4,5},{5,4},{6,7},{7,6},{8,9},{9,8},{10,11... | collective-permute-start | bytes 1572872 | tf_op jit(solution)/shard_map/ppermute | solution.py:143
  64.3 1.9 %collective-permute-done.3.received = f32[16,2,2,16,128]{4,3,2,1,0:T(8,128)S(1)} collective-permute-done((f32[16,2,2,16,128]{4,3,2,1,0:T(8,128)S(1)}, f32[16,2,2,16,128]{4,3,2,1,0:T(8,128)S(1)}, u32[]{:S(2)}, u32[]{:S(2)}) %collective-permute-start.3) | collective-permute-done | bytes 524320 | tf_op jit(solution)/shard_map/ppermute | solution.py:143
  66.1 1.6 %shard_map.52 = (f32[16,2,16,128]{3,2,1,0:T(8,128)S(1)}, f32[16,2,16,128]{3,2,1,0:T(8,128)S(1)}) custom-call(s32[4]{0:T(128)S(1)} %pad_add_fusion.index, bf16[1024,1536]{1,0:T(8,128)(2,1)S(1)} %bitcast.19, f32[16,2,2,16,128]{4,3,2,1,0:T(8,128)S(1)} %collective-permute-done.3.received), custom_call_target="tpu_custom_call" | custom-call | flops 805306368 | bytes 8388608 | tf_op jit(solution)/shard_map/pallas_call | solution.py:144
  67.7 2.1 %collective-permute-start.5 = (bf16[1024,1536]{1,0:T(8,128)(2,1)S(1)}, bf16[1024,1536]{1,0:T(8,128)(2,1)S(1)}, u32[]{:S(2)}, u32[]{:S(2)}) collective-permute-start(bf16[1024,1536]{1,0:T(8,128)(2,1)S(1)} %bitcast.20), channel_id=1, source_target_pairs={{0,1},{1,0},{2,3},{3,2},{4,5},{5,4},{6,7},{7,6},{8,9},{9,8},{10,11... | collective-permute-start | bytes 9437192 | tf_op jit(solution)/shard_map/ppermute | solution.py:154
  69.8 3.0 %collective-permute-start.4 = (f32[16,2,16,128]{3,2,1,0:T(8,128)S(1)}, f32[16,2,16,128]{3,2,1,0:T(8,128)S(1)}, u32[]{:S(2)}, u32[]{:S(2)}) collective-permute-start(f32[16,2,16,128]{3,2,1,0:T(8,128)S(1)} %get-tuple-element.25), channel_id=1, source_target_pairs={{0,16},{16,0},{1,17},{17,1},{2,18},{18,2},{3,19},{19,3},{4,20},{20... | collective-permute-start | bytes 786440 | tf_op jit(solution)/shard_map/ppermute | solution.py:153
  72.8 1.4 %shard_map.53.factor = bf16[1024,128]{1,0:T(8,128)(2,1)S(1)} custom-call(s32[4]{0:T(128)S(1)} %pad_add_fusion.index, bf16[512,128]{1,0:T(8,128)(2,1)S(1)} %all_gather.3.h, bf16[512,128]{1,0:T(8,128)(2,1)} %collective-permute-done.2.h_yl, bf16[512,128]{1,0:T(8,128)(2,1)S(1)} %collective-permute-done.1.h_yh, bf16[512,128]{1,0:T(8,128)(2,1)S(1)} %collective-permute-done.h_both), custom_call_target="tpu_custom_call" | custom-call | bytes 1048576 | tf_op jit(solution)/shard_map/pallas_call | solution.py:155
  74.2 0.6 shard_map.54.here
  74.9 0.4 collective-permute-done.5.rows
  75.3 0.0 copy-start
  75.3 1.1 shard_map.55
  76.4 3.8 %collective-permute-done.4 = f32[16,2,16,128]{3,2,1,0:T(8,128)S(1)} collective-permute-done((f32[16,2,16,128]{3,2,1,0:T(8,128)S(1)}, f32[16,2,16,128]{3,2,1,0:T(8,128)S(1)}, u32[]{:S(2)}, u32[]{:S(2)}) %collective-permute-start.4) | collective-permute-done | bytes 262176 | tf_op jit(solution)/shard_map/ppermute | solution.py:153
  80.3 0.7 add.40
  81.0 9.2 %all-to-all-start.1 = ((f32[16,2,16,128]{3,2,1,0:T(8,128)}), f32[16,2,16,128]{3,2,1,0:T(8,128)S(1)}, u32[]{:S(2)}, u32[]{:S(2)}) async-start(f32[16,2,16,128]{3,2,1,0:T(8,128)} %add.40), calls=%async_computation.1 | async-start | bytes 524288 | tf_op jit(solution)/shard_map/all_to_all | solution.py:183
  90.3 3.3 %collective-permute-start.6 = (f32[64,3072]{1,0:T(8,128)S(1)}, f32[64,3072]{1,0:T(8,128)S(1)}, u32[]{:S(2)}, u32[]{:S(2)}) collective-permute-start(f32[64,3072]{1,0:T(8,128)S(1)} %get-tuple-element.31), channel_id=1, source_target_pairs={{0,8},{8,0},{1,9},{9,1},{2,10},{10,2},{3,11},{11,3},{4,12},{12,4},... | collective-permute-start | bytes 2359304 | tf_op jit(solution)/shard_map/ppermute | solution.py:179
  93.6 0.1 compare_select_fusion
  93.7 0.0 copy-done
  93.7 1.5 %shard_map.56.polar_in = f32[2,64,3072]{2,1,0:T(8,128)} custom-call(s32[4]{0:T(128)S(1)} %pad_add_fusion.index, bf16[2,64,3072]{2,1,0:T(8,128)(2,1)S(1)} %copy-done, f32[64,3072]{1,0:T(8,128)S(1)} %get-tuple-element.34.keep), custom_call_target="tpu_custom_call" | custom-call | flops 196608 | bytes 1966080 | tf_op jit(solution)/shard_map/pallas_call | solution.py:186
  95.2 13.3 %all-to-all-done.1 = f32[16,2,16,128]{3,2,1,0:T(8,128)S(1)} async-done(((f32[16,2,16,128]{3,2,1,0:T(8,128)}), f32[16,2,16,128]{3,2,1,0:T(8,128)S(1)}, u32[]{:S(2)}, u32[]{:S(2)}) %all-to-all-start.1) | async-done | bytes 262176 | tf_op jit(solution)/shard_map/all_to_all | solution.py:183
  108.6 3.3 %collective-permute-start.7 = (f32[16,128]{1,0:T(8,128)S(1)}, f32[16,128]{1,0:T(8,128)S(1)}, u32[]{:S(2)}, u32[]{:S(2)}) collective-permute-start(f32[16,128]{1,0:T(8,128)S(1)} %get-tuple-element.41), channel_id=1, source_target_pairs={{0,8},{8,0},{1,9},{9,1},{2,10},{10,2},{3,11},{11,3},{4,12},{12,4},... | collective-permute-start | bytes 24584 | tf_op jit(solution)/shard_map/ppermute | solution.py:201
  111.9 0.6 collective-permute-done.6.recon
  112.5 1.5 %shard_map.57 = f32[2,64,3072]{2,1,0:T(8,128)} custom-call(s32[4]{0:T(128)S(1)} %pad_add_fusion.index, bf16[2,64,3072]{2,1,0:T(8,128)(2,1)S(1)} %copy-done, f32[64,3072]{1,0:T(8,128)S(1)} %collective-permute-done.6.recon, f32[2,64,3072]{2,1,0:T(8,128)} %shard_map.56.polar_in), custom_call_target="tpu_custom_call", output_to_operand_aliasing={{}: (3, {})} | custom-call | flops 196608 | bytes 1966080 | tf_op jit(solution)/shard_map/pallas_call | solution.py:186
  113.9 0.1 broadcast_in_dim.42
  114.0 1.6 %collective-permute-done.7 = f32[16,128]{1,0:T(8,128)S(1)} collective-permute-done((f32[16,128]{1,0:T(8,128)S(1)}, f32[16,128]{1,0:T(8,128)S(1)}, u32[]{:S(2)}, u32[]{:S(2)}) %collective-permute-start.7) | collective-permute-done | bytes 8224 | tf_op jit(solution)/shard_map/ppermute | solution.py:201
  115.6 0.1 broadcast_in_dim.46
  115.7 0.7 subtract_multiply_fusion
  (8 shorter events, 0.1 us)
Async XLA Ops:
  3.4 9.4 %copy-start.1 = (bf16[2,32,64]{2,1,0:T(8,128)(2,1)S(1)}, bf16[2,32,64]{2,1,0:T(8,128)(2,1)}, u32[]{:S(2)}) copy-start(bf16[2,32,64]{2,1,0:T(8,128)(2,1)} %param.5) | copy-start | bytes 24580
  3.4 57.4 %all-to-all-start = ((bf16[16,64,1536]{2,1,0:T(8,128)(2,1)}), bf16[16,64,1536]{2,1,0:T(8,128)(2,1)S(1)}, u32[]{:S(2)}, u32[]{:S(2)}) async-start(bf16[16,64,1536]{2,1,0:T(8,128)(2,1)} %bitcast.22), calls=%async_computation | async-start | bytes 6291456 | tf_op jit(solution)/shard_map/all_to_all | solution.py:121
  47.0 9.9 %collective-permute-start = (bf16[512,128]{1,0:T(8,128)(2,1)S(1)}, bf16[512,128]{1,0:T(8,128)(2,1)S(1)}, u32[]{:S(2)}, u32[]{:S(2)}) collective-permute-start(bf16[512,128]{1,0:T(8,128)(2,1)S(1)} %all_gather.3.h), channel_id=1, source_target_pairs={{0,24},{8,16},{16,8},{24,0},{1,25},{9,17},{17,9},{25,1},{2,26},{10... | collective-permute-start | bytes 393224 | tf_op jit(solution)/shard_map/ppermute | solution.py:123
  51.7 8.4 %collective-permute-start.1 = (bf16[512,128]{1,0:T(8,128)(2,1)S(1)}, bf16[512,128]{1,0:T(8,128)(2,1)S(1)}, u32[]{:S(2)}, u32[]{:S(2)}) collective-permute-start(bf16[512,128]{1,0:T(8,128)(2,1)S(1)} %all_gather.3.h), channel_id=1, source_target_pairs={{0,8},{8,0},{1,9},{9,1},{2,10},{10,2},{3,11},{11,3},{4,12},{12,4},... | collective-permute-start | bytes 393224 | tf_op jit(solution)/shard_map/ppermute | solution.py:124
  53.8 7.0 %collective-permute-start.2 = (bf16[512,128]{1,0:T(8,128)(2,1)S(1)}, bf16[512,128]{1,0:T(8,128)(2,1)}, u32[]{:S(2)}, u32[]{:S(2)}) collective-permute-start(bf16[512,128]{1,0:T(8,128)(2,1)S(1)} %all_gather.3.h), channel_id=1, source_target_pairs={{0,16},{16,0},{1,17},{17,1},{2,18},{18,2},{3,19},{19,3},{4,20},{20... | collective-permute-start | bytes 393224 | tf_op jit(solution)/shard_map/ppermute | solution.py:125
  62.3 3.8 %collective-permute-start.3 = (f32[16,2,2,16,128]{4,3,2,1,0:T(8,128)S(1)}, f32[16,2,2,16,128]{4,3,2,1,0:T(8,128)S(1)}, u32[]{:S(2)}, u32[]{:S(2)}) collective-permute-start(f32[16,2,2,16,128]{4,3,2,1,0:T(8,128)S(1)} %shard_map.51), channel_id=1, source_target_pairs={{0,1},{1,0},{2,3},{3,2},{4,5},{5,4},{6,7},{7,6},{8,9},{9,8},{10,11... | collective-permute-start | bytes 1572872 | tf_op jit(solution)/shard_map/ppermute | solution.py:143
  67.7 7.6 %collective-permute-start.5 = (bf16[1024,1536]{1,0:T(8,128)(2,1)S(1)}, bf16[1024,1536]{1,0:T(8,128)(2,1)S(1)}, u32[]{:S(2)}, u32[]{:S(2)}) collective-permute-start(bf16[1024,1536]{1,0:T(8,128)(2,1)S(1)} %bitcast.20), channel_id=1, source_target_pairs={{0,1},{1,0},{2,3},{3,2},{4,5},{5,4},{6,7},{7,6},{8,9},{9,8},{10,11... | collective-permute-start | bytes 9437192 | tf_op jit(solution)/shard_map/ppermute | solution.py:154
  69.8 10.5 %collective-permute-start.4 = (f32[16,2,16,128]{3,2,1,0:T(8,128)S(1)}, f32[16,2,16,128]{3,2,1,0:T(8,128)S(1)}, u32[]{:S(2)}, u32[]{:S(2)}) collective-permute-start(f32[16,2,16,128]{3,2,1,0:T(8,128)S(1)} %get-tuple-element.25), channel_id=1, source_target_pairs={{0,16},{16,0},{1,17},{17,1},{2,18},{18,2},{3,19},{19,3},{4,20},{20... | collective-permute-start | bytes 786440 | tf_op jit(solution)/shard_map/ppermute | solution.py:153
  75.3 18.4 %copy-start = (bf16[2,64,3072]{2,1,0:T(8,128)(2,1)S(1)}, bf16[2,64,3072]{2,1,0:T(8,128)(2,1)}, u32[]{:S(2)}) copy-start(bf16[2,64,3072]{2,1,0:T(8,128)(2,1)} %target.3) | copy-start | bytes 2359300
  81.0 27.5 %all-to-all-start.1 = ((f32[16,2,16,128]{3,2,1,0:T(8,128)}), f32[16,2,16,128]{3,2,1,0:T(8,128)S(1)}, u32[]{:S(2)}, u32[]{:S(2)}) async-start(f32[16,2,16,128]{3,2,1,0:T(8,128)} %add.40), calls=%async_computation.1 | async-start | bytes 524288 | tf_op jit(solution)/shard_map/all_to_all | solution.py:183
  90.3 22.2 %collective-permute-start.6 = (f32[64,3072]{1,0:T(8,128)S(1)}, f32[64,3072]{1,0:T(8,128)S(1)}, u32[]{:S(2)}, u32[]{:S(2)}) collective-permute-start(f32[64,3072]{1,0:T(8,128)S(1)} %get-tuple-element.31), channel_id=1, source_target_pairs={{0,8},{8,0},{1,9},{9,1},{2,10},{10,2},{3,11},{11,3},{4,12},{12,4},... | collective-permute-start | bytes 2359304 | tf_op jit(solution)/shard_map/ppermute | solution.py:179
  108.6 7.0 %collective-permute-start.7 = (f32[16,128]{1,0:T(8,128)S(1)}, f32[16,128]{1,0:T(8,128)S(1)}, u32[]{:S(2)}, u32[]{:S(2)}) collective-permute-start(f32[16,128]{1,0:T(8,128)S(1)} %get-tuple-element.41), channel_id=1, source_target_pairs={{0,8},{8,0},{1,9},{9,1},{2,10},{10,2},{3,11},{11,3},{4,12},{12,4},... | collective-permute-start | bytes 24584 | tf_op jit(solution)/shard_map/ppermute | solution.py:201
